TPU v7x, 128 devices: a whole 4x4x4 slice. The times are simulated.
128 devices in a mesh: comp: 2 (over core), tile: 64 (over x, y, z).
Axes of the slice: x: 4, y: 4, z: 4, core: 2. Of those that a mesh axis runs over, the one named last changes fastest.
Arguments:
- surface: float32 [2, 8, 8192, 128], P('comp', None, 'tile'), may hold values from -2.5 to 6, as said below
- area: float32 [2, 8192, 128], P('comp', 'tile'), may hold values from 0.25 to 9, as said below
- sea: int32 [8192, 128], P('tile'), may hold values 0 or 1
- weights: float32 [2, 16384, 128, 128], P('comp', 'tile'), may hold values from 0 to 0.015625
- src_row: int32 [2, 16384], P('comp', 'tile'), may hold values from 0 to 127
- dst_tile: int32 [2, 16384, 1], P('comp', 'tile'), may hold values from 0 to 63; in each aligned block of 256 rows (0 to 255, 256 to 511, ..., all dimensions but the last counted through in order) at most 8 rows name the same one
- dst_local: int32 [2, 16384], P('comp', 'tile'), may hold values from 0 to 127
Outputs:
- remapped: float32 [2, 8, 8192, 128], P('comp', None, 'tile')
Inputs may be any that keep to these rules, and one draw needn't show every extreme that they name: `surface`: each component's fields, of order one with a mean for each field. `area`: positive cell areas. `dst_tile`: the weight blocks held by one tile aim at most 8 blocks at one target tile.
All inputs are finite; a program needn't handle non-finite values. No bound on the sum of `sea` on one device may be relied on, other than what follows from the above.
Results may differ from a plain program's by a relative error of at most 0.0001.
Values sent between devices are 32-bit elements; how exact they have to be, the bound alone decides.
No kernel may reach another device: no remote copies, remote signals or barrier semaphores. Data moves between devices by JAX's collectives and lax.ppermute only.
A program may use at most 64 MiB of HBM per device.

v0:
```python
import jax
import jax.numpy as jnp
from jax import lax
from jax.sharding import PartitionSpec as P

smooth_rate = 0.2


def extended(array, sides, width):
    for axis, dim in sides:
        size, length = (lax.axis_size(axis), array.shape[dim])
        up = [(i, (i + 1) % size) for i in range(size - 1)]
        down = [(j, i) for i, j in up]
        last = lax.slice_in_dim(array, length - width, length, axis=dim)
        first = lax.slice_in_dim(array, 0, width, axis=dim)
        before = lax.ppermute(last, axis, up)
        after = lax.ppermute(first, axis, down)
        array = jnp.concatenate([before, array, after], axis=dim)
    return array


def from_partner(block, axis, stride):
    count = lax.axis_size(axis)
    route = []
    for low in range(count):
        high = low | 1 << stride
        if high != low and high < count:
            route += [(low, high), (high, low)]
    return lax.ppermute(block, axis, route)


def smooth_tile(own_field):
    padded = extended(own_field, (("tile", 1),), 1)
    sides = jnp.pad(own_field, ((0, 0), (0, 0), (1, 1)))
    beside_all = padded[:, :-2] + padded[:, 2:] + sides[:, :, :-2] + sides[:, :, 2:]
    return own_field + smooth_rate * (beside_all - 4.0 * own_field)


def pack_slots(products, tile_of, local_of, tile_count, slot_count):
    matches = (tile_of[:, None] == jnp.arange(tile_count, dtype=jnp.int32)[None, :]).astype(
        jnp.int32
    )
    earlier = jnp.cumsum(matches, axis=0) - matches
    slot_rank = jnp.sum(earlier * matches, axis=1)
    slot_of = tile_of * slot_count + slot_rank
    placing = slot_of[None, :] == jnp.arange(tile_count * slot_count, dtype=jnp.int32)[:, None]
    packed = jnp.einsum(
        "sk,kfd->sfd", placing.astype(jnp.float32), products, precision=lax.Precision.HIGHEST
    )
    target = jnp.sum(jnp.where(placing, local_of[None, :] + 1, 0), axis=1) - 1
    field_count, cell_count = (products.shape[1], products.shape[2])
    return (
        packed.reshape(tile_count, slot_count, field_count, cell_count),
        target.reshape(tile_count, slot_count),
    )


def gather_rows(packed, target, row_count):
    flat_slots = packed.reshape(-1, packed.shape[2], packed.shape[3])
    flat_target = target.reshape(-1)
    placing = (flat_target[None, :] == jnp.arange(row_count, dtype=jnp.int32)[:, None]).astype(
        jnp.float32
    )
    return jnp.einsum("rs,sfd->frd", placing, flat_slots, precision=lax.Precision.HIGHEST)


def shards(surface, area, sea, weights, src_row, dst_tile, dst_local):
    section = lax.axis_index("comp")
    tile_count = lax.axis_size("tile")
    own_field = surface[0]
    row_count = own_field.shape[1]
    block_count = weights.shape[1]
    slot_count = 2 * block_count // tile_count
    smoothed = smooth_tile(own_field)
    own_area = area[0]
    side_vec = (jnp.arange(2, dtype=jnp.int32) == section).astype(jnp.float32)
    own_mask = jnp.where(section == 0, 1.0, sea.astype(jnp.float32))
    source_terms = side_vec[:, None] * jnp.sum(own_area[None] * smoothed, axis=(1, 2))[None, :]
    source_total = lax.psum(source_terms, ("comp", "tile"))
    picked = jnp.take(smoothed, src_row[0], axis=1)
    products = jnp.einsum("fkc,kdc->kfd", picked, weights[0], precision=lax.Precision.HIGHEST)
    packed, target = pack_slots(products, dst_tile[0, :, 0], dst_local[0], tile_count, slot_count)
    packed, target = from_partner((packed, target), "comp", 0)
    packed, target = (
        lax.all_to_all(packed, "tile", split_axis=0, concat_axis=0, tiled=True),
        lax.all_to_all(target, "tile", split_axis=0, concat_axis=0, tiled=True),
    )
    received = gather_rows(packed, target, row_count)
    masked = received * own_mask[None]
    target_terms = side_vec[:, None] * jnp.sum(own_area[None] * masked, axis=(1, 2))[None, :]
    area_terms = side_vec * jnp.sum(own_area * own_mask)
    target_total, area_total = lax.psum((target_terms, area_terms), ("comp", "tile"))
    other_vec = 1.0 - side_vec
    deficit = (
        jnp.sum(source_total * other_vec[:, None], axis=0)
        - jnp.sum(target_total * side_vec[:, None], axis=0)
    ) / jnp.sum(area_total * side_vec)
    return (masked + own_mask[None] * deficit[:, None, None])[None]


def solution(mesh):
    placed = (
        P("comp", None, "tile", None),
        P("comp", "tile", None),
        P("tile", None),
        P("comp", "tile", None, None),
        P("comp", "tile"),
        P("comp", "tile", None),
        P("comp", "tile"),
    )
    return jax.shard_map(
        shards, mesh=mesh, in_specs=placed, out_specs=P("comp", None, "tile", None), check_vma=False
    )
```

profile of v0, /device:TPU:1, one launch (start us, length us, event | category | flops | bytes accessed | tf_op | source)
XLA Modules:
  0.0 182.6 jit_solution(7227550830421042634)
XLA Ops:
  0.0 0.0 copy-start.3
  0.0 0.0 copy-start.2
  0.0 1.3 copy.32
  1.3 0.2 fusion.34
  1.5 4.4 %collective-permute-start = (f32[8,1,128]{1,2,0:T(8,128)S(1)}, f32[8,1,128]{1,2,0:T(8,128)S(1)}, u32[]{:S(2)}, u32[]{:S(2)}) collective-permute-start(f32[8,1,128]{1,2,0:T(8,128)S(1)} %get-tuple-element.12), channel_id=1, source_target_pairs={{0,1},{1,2},{2,3},{3,4},{4,5},{5,6},{6,7},{7,8},{8,9},{9,10},{10,1... | collective-permute-start | bytes 12296 | tf_op jit(solution)/shard_map/ppermute | solution.py:16
  5.9 1.3 collective-permute-start.1
  7.2 0.0 copy-done.3
  7.2 0.0 copy-done.2
  7.3 0.6 reduce-window.6
  7.9 0.2 slice_reduce_fusion
  8.1 0.1 fusion.29
  8.2 8.2 %collective-permute-done = f32[8,1,128]{1,2,0:T(8,128)S(1)} collective-permute-done((f32[8,1,128]{1,2,0:T(8,128)S(1)}, f32[8,1,128]{1,2,0:T(8,128)S(1)}, u32[]{:S(2)}, u32[]{:S(2)}) %collective-permute-start) | collective-permute-done | bytes 4128 | tf_op jit(solution)/shard_map/ppermute | solution.py:16
  16.4 4.2 %collective-permute-done.1 = f32[8,1,128]{1,2,0:T(8,128)S(1)} collective-permute-done((f32[8,1,128]{1,2,0:T(8,128)S(1)}, f32[8,1,128]{1,2,0:T(8,128)S(1)}, u32[]{:S(2)}, u32[]{:S(2)}) %collective-permute-start.1) | collective-permute-done | bytes 4128 | tf_op jit(solution)/shard_map/ppermute | solution.py:17
  20.6 0.5 fusion.17
  21.1 0.2 copy.33
  21.3 1.0 gather_fusion
  22.3 28.8 %fusion = f32[256,8,128]{2,1,0:T(8,128)S(1)} fusion(f32[1,256,128,128]{3,2,1,0:T(8,128)} %param.10, f32[256,8,128]{2,1,0:T(8,128)S(1)} %gather_fusion, pred[256]{0:T(512)(128)(4,1)S(1)} %compare_and_fusion), kind=kOutput, calls=%fused_computation.1 | convolution fusion | flops 402915328 | bytes 18874624 | tf_op jit(solution)/shard_map/fkc,kdc->kfd/dot_general | solution.py:81
  51.1 1.2 convolution_bitcast_fusion
  52.3 0.0 copy-start.4
  52.3 1.2 copy.35
  53.5 1.8 collective-permute-start.2
  55.3 0.0 copy-done.4
  55.3 0.2 select_reduce_fusion
  55.5 0.1 sub.29
  55.6 0.1 collective-permute-start.3
  55.7 3.5 %collective-permute-done.3 = s32[64,8]{1,0:T(8,128)S(1)} collective-permute-done((s32[64,8]{1,0:T(8,128)S(1)}, s32[64,8]{1,0:T(8,128)S(1)}, u32[]{:S(2)}, u32[]{:S(2)}) %collective-permute-start.3) | collective-permute-done | bytes 2080 | tf_op jit(solution)/shard_map/ppermute | solution.py:29
  59.1 21.6 %all_to_all.14 = s32[64,1,8]{2,1,0:T(1,128)S(1)} all-to-all(s32[64,1,8]{2,1,0:T(1,128)S(1)} %bitcast.59), channel_id=1, replica_groups=mesh['comp'=2,'tile'=64] {'tile'}, dimensions={0} | all-to-all | bytes 4096 | tf_op jit(solution)/shard_map/all_to_all | solution.py:86
  80.7 0.0 copy-start
  80.7 0.0 collective-permute-done.2
  80.7 5.0 %all-to-all-start = ((f32[64,8,8,128]{3,2,1,0:T(8,128)}), f32[64,8,8,128]{3,2,1,0:T(8,128)S(1)}, u32[]{:S(2)}, u32[]{:S(2)}) async-start(f32[64,8,8,128]{3,2,1,0:T(8,128)} %collective-permute-done.2), calls=%async_computation | async-start | bytes 4194304 | tf_op jit(solution)/shard_map/all_to_all | solution.py:85
  85.7 0.0 copy-done
  85.7 0.0 copy-done.1
  85.7 0.6 multiply_reduce_fusion.2
  86.3 0.1 copy.38
  86.4 0.1 copy.39
  86.6 0.7 fusion.31
  87.2 0.5 broadcast.105
  87.7 0.7 reduce.5
  88.5 0.1 eq.77
  88.6 23.3 %all-to-all-done = f32[64,8,8,128]{3,2,1,0:T(8,128)S(1)} async-done(((f32[64,8,8,128]{3,2,1,0:T(8,128)}), f32[64,8,8,128]{3,2,1,0:T(8,128)S(1)}, u32[]{:S(2)}, u32[]{:S(2)}) %all-to-all-start) | async-done | bytes 2097184 | tf_op jit(solution)/shard_map/all_to_all | solution.py:85
  111.9 1.9 %multiply_reduce_fusion = (f32[8]{0:T(128)S(1)}, f32[8]{0:T(128)S(1)}, f32[8,128,128]{1,2,0:T(8,128)S(1)}) fusion(f32[128,128]{0,1:T(8,128)S(1)} %copy.39, f32[8,128,128]{1,2,0:T(8,128)S(1)} %fusion.17, f32[128,128]{0,1:T(8,128)S(1)} %copy.38, s32[512]{0:T(512)S(1)} %eq.77, f32[512,8,128]{2,1,0:T(8,128)S(1)} %bitcast.55), kind=kOutput, calls=%fused_computation.23 | convolution fusion | flops 806027264 | bytes 3278912 | tf_op jit(solution)/shard_map/rs,sfd->frd/dot_general | solution.py:64
  113.8 0.1 broadcast_multiply_fusion
  113.9 66.3 %all-reduce.1 = (f32[2,8]{1,0:T(2,128)S(1)}, f32[2,8]{1,0:T(2,128)S(1)}, f32[2]{0:T(128)S(1)}) all-reduce(f32[2,8]{1,0:T(2,128)S(1)} %get-tuple-element.15, f32[2,8]{1,0:T(2,128)S(1)} %get-tuple-element.14, f32[2]{0:T(128)S(1)} %fusion.31), channel_id=1, replica_groups=mesh['comp'=2,'tile'=64] {'comp','tile'}, use_global_device_ids=true, to_apply=%region_5.6 | all-reduce | flops 34 | bytes 272 | tf_op jit(solution)/shard_map/psum | solution.py:79
  180.1 0.6 select_reduce_fusion.1
  180.7 0.1 multiply_reduce_fusion.3
  180.8 0.6 subtract_divide_fusion
  181.5 0.1 add_bitcast_fusion
  181.6 1.0 copy.40
  (12 shorter events, 0.1 us)
Async XLA Ops:
  0.0 7.2 %copy-start.3 = (s32[1,256]{1,0:T(1,128)S(1)}, s32[1,256]{1,0:T(1,128)}, u32[]{:S(2)}) copy-start(s32[1,256]{1,0:T(1,128)} %param.11) | copy-start | bytes 3076
  0.0 7.2 %copy-start.2 = (s32[1,256,1]{1,2,0:T(1,128)S(1)}, s32[1,256,1]{1,2,0:T(1,128)}, u32[]{:S(2)}) copy-start(s32[1,256,1]{1,2,0:T(1,128)} %param.12) | copy-start | bytes 3076
  1.5 15.0 %collective-permute-start = (f32[8,1,128]{1,2,0:T(8,128)S(1)}, f32[8,1,128]{1,2,0:T(8,128)S(1)}, u32[]{:S(2)}, u32[]{:S(2)}) collective-permute-start(f32[8,1,128]{1,2,0:T(8,128)S(1)} %get-tuple-element.12), channel_id=1, source_target_pairs={{0,1},{1,2},{2,3},{3,4},{4,5},{5,6},{6,7},{7,8},{8,9},{9,10},{10,1... | collective-permute-start | bytes 12296 | tf_op jit(solution)/shard_map/ppermute | solution.py:16
  5.9 14.7 %collective-permute-start.1 = (f32[8,1,128]{1,2,0:T(8,128)S(1)}, f32[8,1,128]{1,2,0:T(8,128)S(1)}, u32[]{:S(2)}, u32[]{:S(2)}) collective-permute-start(f32[8,1,128]{1,2,0:T(8,128)S(1)} %get-tuple-element.13), channel_id=1, source_target_pairs={{1,0},{2,1},{3,2},{4,3},{5,4},{6,5},{7,6},{8,7},{9,8},{10,9},{11,1... | collective-permute-start | bytes 12296 | tf_op jit(solution)/shard_map/ppermute | solution.py:17
  52.3 3.0 %copy-start.4 = (s32[1,256]{1,0:T(1,128)S(1)}, s32[1,256]{1,0:T(1,128)}, u32[]{:S(2)}) copy-start(s32[1,256]{1,0:T(1,128)} %param.13) | copy-start | bytes 3076
  53.5 27.2 %collective-permute-start.2 = (f32[64,8,8,128]{3,2,1,0:T(8,128)S(1)}, f32[64,8,8,128]{3,2,1,0:T(8,128)}, u32[]{:S(2)}, u32[]{:S(2)}) collective-permute-start(f32[64,8,8,128]{3,2,1,0:T(8,128)S(1)} %copy.35), channel_id=1, source_target_pairs={{0,64},{64,0},{1,65},{65,1},{2,66},{66,2},{3,67},{67,3},{4,68},{68... | collective-permute-start | bytes 6291464 | tf_op jit(solution)/shard_map/ppermute | solution.py:29
  55.6 3.6 %collective-permute-start.3 = (s32[64,8]{1,0:T(8,128)S(1)}, s32[64,8]{1,0:T(8,128)S(1)}, u32[]{:S(2)}, u32[]{:S(2)}) collective-permute-start(s32[64,8]{1,0:T(8,128)S(1)} %sub.29), channel_id=1, source_target_pairs={{0,64},{64,0},{1,65},{65,1},{2,66},{66,2},{3,67},{67,3},{4,68},{68... | collective-permute-start | bytes 6152 | tf_op jit(solution)/shard_map/ppermute | solution.py:29
  80.7 5.0 %copy-start = (f32[1,128,128]{2,1,0:T(8,128)S(1)}, f32[1,128,128]{2,1,0:T(8,128)}, u32[]{:S(2)}) copy-start(f32[1,128,128]{2,1,0:T(8,128)} %param.8) | copy-start | bytes 196612
  80.7 5.0 %copy-start.1 = (s32[128,128]{1,0:T(8,128)S(1)}, s32[128,128]{1,0:T(8,128)}, u32[]{:S(2)}) copy-start(s32[128,128]{1,0:T(8,128)} %param.9) | copy-start | bytes 196612
  80.7 31.2 %all-to-all-start = ((f32[64,8,8,128]{3,2,1,0:T(8,128)}), f32[64,8,8,128]{3,2,1,0:T(8,128)S(1)}, u32[]{:S(2)}, u32[]{:S(2)}) async-start(f32[64,8,8,128]{3,2,1,0:T(8,128)} %collective-permute-done.2), calls=%async_computation | async-start | bytes 4194304 | tf_op jit(solution)/shard_map/all_to_all | solution.py:85
where the time goes:
time: 183 us
  blocking collectives  87.8 us (48%)
  waiting for transfers between devices  39.1 us (21%)
  matrix products  31.9 us (17%)
  starting transfers between devices  12.6 us (7%)
  local copies, waits for them, and re-layouts  6.02 us (3%)
  other arithmetic  4.95 us (3%)
    psum x1, blocking collectives, shards(): source_total = lax.psum(source_terms, ('comp', 'tile'))  66.3 us
    dot_general x1, matrix products, shards(): jnp.einsum('fkc,kdc->kfd', picked, weights[0], precision=lax.Precision.HI...  28.8 us
    all_to_all x1, waiting for transfers between devices, shards(): lax.all_to_all(packed, 'tile', split_axis=0, concat_axis=0, tiled=True)  23.3 us
    all_to_all x1, blocking collectives, shards(): lax.all_to_all(target, 'tile', split_axis=0, concat_axis=0, tiled=True)  21.6 us
    ppermute x1, waiting for transfers between devices, extended(): before = lax.ppermute(last, axis, up)  8.2 us
    all_to_all x1, starting transfers between devices, shards(): lax.all_to_all(packed, 'tile', split_axis=0, concat_axis=0, tiled=True)  5.01 us
    ppermute x1, starting transfers between devices, extended(): before = lax.ppermute(last, axis, up)  4.4 us
    ppermute x1, waiting for transfers between devices, extended(): after = lax.ppermute(first, axis, down)  4.16 us
  transfers between devices with their start and end apart: 5, of which 4 were waited for; matrix products, arithmetic and copies ran while one was open for 2% of the time, Pallas kernels for 0%

commit v1 on v0

v1 whole, which is shorter than its diff:
```python
import functools

import jax
import jax.numpy as jnp
from jax import lax
from jax.experimental import pallas as pl
from jax.experimental.pallas import tpu as pltpu
from jax.sharding import PartitionSpec as P

RATE = 0.2
LANES = 128
SUB = 8
CHUNKS = 16
EDGES = 16

F32 = jnp.float32
BF16 = jnp.bfloat16
I32 = jnp.int32


def split_rows(rows):
    lead = rows.astype(BF16).astype(F32)
    return jnp.concatenate([lead, rows - lead], axis=0).astype(BF16)


def block_product(rows2, w):
    lead = w.astype(BF16)
    rest = (w - lead.astype(F32)).astype(BF16)
    dims = (((1,), (1,)), ((), ()))
    a = lax.dot_general(rows2, lead, dims, preferred_element_type=F32)
    b = lax.dot_general(rows2, rest, dims, preferred_element_type=F32)
    t = a + b
    return t[:SUB] + t[SUB:]


def products_kernel(
    row_ref, surf_ref, area_ref, w_ref,
    prod_ref, part_ref, edge_w_ref, edge_ref,
    wbuf, smooth, rows2, sems, *, blocks, fields, rows,
):
    per = blocks // CHUNKS

    def fetch(c):
        span = pl.ds(c * per, per)
        return pltpu.make_async_copy(w_ref.at[0, span], wbuf.at[span], sems.at[c])

    for c in range(CHUNKS):
        fetch(c).start()

    r_iota = lax.broadcasted_iota(I32, (rows, LANES), 0)
    c_iota = lax.broadcasted_iota(I32, (rows, LANES), 1)
    area = area_ref[0]
    for f in range(fields):
        s = surf_ref[0, f]
        n = jnp.where(r_iota > 0, pltpu.roll(s, 1, 0), 0.0)
        n += jnp.where(r_iota < rows - 1, pltpu.roll(s, rows - 1, 0), 0.0)
        n += jnp.where(c_iota > 0, pltpu.roll(s, 1, 1), 0.0)
        n += jnp.where(c_iota < LANES - 1, pltpu.roll(s, LANES - 1, 1), 0.0)
        sm = s + RATE * (n - 4.0 * s)
        part_ref[pl.ds(f, 1), :] = jnp.sum(area * sm, axis=0, keepdims=True)
        smooth[pl.ds(f, rows, stride=fields), :] = sm

    def halves(g, carry):
        rows2[g] = split_rows(smooth[pl.ds(pl.multiple_of(g * SUB, SUB), SUB), :])
        return carry

    lax.fori_loop(0, rows, halves, 0, unroll=8)

    def chunk(c, n_edge):
        fetch(c).wait()
        for b in range(per):
            k = c * per + b
            g = row_ref[0, k]
            edge_ref[n_edge] = k
            n_edge += jnp.logical_or(g == 0, g == rows - 1).astype(I32)
            at = pl.multiple_of(k * SUB, SUB)
            prod_ref[pl.ds(at, SUB), :] = block_product(rows2[g], wbuf[k])
        return n_edge

    n_edge = lax.fori_loop(0, CHUNKS, chunk, 0)
    edge_ref[blocks] = n_edge

    def keep(e, carry):
        edge_w_ref[e] = wbuf[edge_ref[e]]
        return carry

    lax.fori_loop(0, jnp.minimum(n_edge, EDGES), keep, 0)


def pack_kernel(
    row_ref, tile_ref, local_ref, edge_ref, prod_ref, part_ref, edge_w_ref, before_ref, after_ref,
    area_ref, w_ref,
    packed_ref, total_ref, wbuf, count, place, sem, *, blocks, fields, rows, slots, tiles,
):
    pitch = (fields + 1) * slots

    def clear(t, carry):
        count[t] = 0
        base = pl.multiple_of(t * pitch + fields * slots, SUB)
        packed_ref[pl.ds(base, slots), :] = jnp.full((slots, LANES), -1.0, F32)
        return carry

    lax.fori_loop(0, tiles, clear, 0, unroll=8)

    def pack(k, carry):
        t = tile_ref[k]
        rank = count[t]
        count[t] = rank + 1
        at = t * pitch + rank
        place[k] = at
        packed_ref[pl.ds(at, fields, stride=slots), :] = prod_ref[pl.ds(pl.multiple_of(k * SUB, SUB), SUB), :]
        local = jnp.full((1, LANES), local_ref[0, k], I32)
        packed_ref[pl.ds(at + fields * slots, 1), :] = local.astype(F32)
        return carry

    lax.fori_loop(0, blocks, pack, 0, unroll=8)

    before = RATE * before_ref[...]
    after = RATE * after_ref[...]
    area = area_ref[0]
    total_ref[...] = part_ref[...] + area[0:1] * before + area[rows - 1 : rows] * after

    def add(e, w):
        k = edge_ref[e]
        halo = jnp.where(row_ref[0, k] == 0, before, after)
        spot = pl.ds(place[k], fields, stride=slots)
        packed_ref[spot, :] = packed_ref[spot, :] + block_product(split_rows(halo), w)

    def near(e, carry):
        add(e, edge_w_ref[e])
        return carry

    def far(e, carry):
        copy = pltpu.make_async_copy(w_ref.at[0, edge_ref[e]], wbuf, sem)
        copy.start()
        copy.wait()
        add(e, wbuf[...])
        return carry

    n_edge = edge_ref[blocks]
    lax.fori_loop(0, jnp.minimum(n_edge, EDGES), near, 0)
    lax.fori_loop(EDGES, n_edge, far, 0)


def place_kernel(
    section_ref, recv_ref, total_ref, area_ref, sea_ref, masked_ref, tail_ref,
    *, fields, rows, slots, tiles,
):
    count = tiles * slots
    target = recv_ref[:, fields * slots :, :].reshape(count, LANES)
    lane = lax.broadcasted_iota(I32, (count, rows), 1).astype(F32)
    placing = jnp.where(target == lane, 1.0, 0.0).T.astype(BF16)
    used = target >= 0.0
    first = section_ref[0] == 1
    mask = jnp.where(first, 1.0, sea_ref[...].astype(F32))
    weight = area_ref[0] * mask
    lane1 = lax.broadcasted_iota(I32, (1, LANES), 1)
    tail = jnp.where(lane1 == fields, jnp.sum(weight), 0.0)
    for f in range(fields):
        x = recv_ref[:, f * slots : (f + 1) * slots, :].reshape(count, LANES)
        x = jnp.where(used, x, 0.0)
        lead = x.astype(BF16)
        rest = (x - lead.astype(F32)).astype(BF16)
        got = jnp.dot(placing, lead, preferred_element_type=F32)
        got += jnp.dot(placing, rest, preferred_element_type=F32)
        masked_ref[f] = got * mask
        gap = jnp.sum(total_ref[pl.ds(f, 1), :]) - jnp.sum(weight * got)
        tail += jnp.where(lane1 == f, gap, 0.0)
    tail_ref[...] = jnp.broadcast_to(tail, (tiles, LANES))


def correct_kernel(section_ref, masked_ref, tail_ref, sea_ref, out_ref, *, fields):
    sums = jnp.sum(tail_ref[...], axis=0, keepdims=True)
    lane1 = lax.broadcasted_iota(I32, (1, LANES), 1)
    whole = jnp.sum(jnp.where(lane1 == fields, sums, 0.0), axis=1, keepdims=True)
    deficit = sums / whole
    first = section_ref[0] == 1
    mask = jnp.where(first, 1.0, sea_ref[...].astype(F32))
    for f in range(fields):
        d = jnp.sum(jnp.where(lane1 == f, deficit, 0.0), axis=1, keepdims=True)
        out_ref[0, f] = masked_ref[f] + mask * d


VMEM = pl.BlockSpec(memory_space=pltpu.VMEM)
SMEM = pl.BlockSpec(memory_space=pltpu.SMEM)
ANY = pl.BlockSpec(memory_space=pl.ANY)


def shards(surface, area, sea, weights, src_row, dst_tile, dst_local):
    tiles = lax.axis_size("tile")
    section = lax.axis_index("comp").astype(I32).reshape(1)
    _, fields, rows, cells = surface.shape
    blocks = weights.shape[1]
    slots = 2 * blocks // tiles
    pitch = (fields + 1) * slots
    swap = [(0, 1), (1, 0)]
    up = [(i, i + 1) for i in range(tiles - 1)]
    down = [(i + 1, i) for i in range(tiles - 1)]

    before = lax.ppermute(surface[0, :, rows - 1], "tile", up)
    after = lax.ppermute(surface[0, :, 0], "tile", down)
    area_far = lax.ppermute(area, "comp", swap)
    tile_of = dst_tile.reshape(blocks)

    sizes = dict(blocks=blocks, rows=rows, slots=slots)
    prod, part, edge_w, edges = pl.pallas_call(
        functools.partial(products_kernel, blocks=blocks, fields=fields, rows=rows),
        out_shape=(
            jax.ShapeDtypeStruct((blocks * fields, LANES), F32),
            jax.ShapeDtypeStruct((fields, LANES), F32),
            jax.ShapeDtypeStruct((EDGES, cells, cells), F32),
            jax.ShapeDtypeStruct((blocks + 8,), I32),
        ),
        in_specs=[SMEM, VMEM, VMEM, ANY],
        out_specs=(VMEM, VMEM, VMEM, SMEM),
        scratch_shapes=[
            pltpu.VMEM((blocks, cells, cells), F32),
            pltpu.VMEM((rows * fields, cells), F32),
            pltpu.VMEM((rows, 2 * SUB, cells), BF16),
            pltpu.SemaphoreType.DMA((CHUNKS,)),
        ],
        compiler_params=pltpu.CompilerParams(vmem_limit_bytes=52 << 20),
        cost_estimate=pl.CostEstimate(flops=2 * 10**8, bytes_accessed=20 << 20, transcendentals=0),
        name="products",
    )(src_row, surface, area, weights)

    packed, total = pl.pallas_call(
        functools.partial(
            pack_kernel, blocks=blocks, fields=fields, rows=rows, slots=slots, tiles=tiles
        ),
        out_shape=(
            jax.ShapeDtypeStruct((tiles * pitch, LANES), F32),
            jax.ShapeDtypeStruct((fields, LANES), F32),
        ),
        in_specs=[SMEM] * 4 + [VMEM] * 6 + [ANY],
        out_specs=(VMEM, VMEM),
        scratch_shapes=[
            pltpu.VMEM((cells, cells), F32),
            pltpu.SMEM((tiles,), I32),
            pltpu.SMEM((blocks,), I32),
            pltpu.SemaphoreType.DMA,
        ],
        compiler_params=pltpu.CompilerParams(vmem_limit_bytes=52 << 20),
        name="pack",
    )(src_row, tile_of, dst_local, edges, prod, part, edge_w, before, after, area, weights)

    recv = lax.all_to_all(packed.reshape(tiles, pitch, LANES), "tile", 0, 0, tiled=True)

    masked, tail = pl.pallas_call(
        functools.partial(place_kernel, fields=fields, rows=rows, slots=slots, tiles=tiles),
        out_shape=(
            jax.ShapeDtypeStruct((fields, rows, cells), F32),
            jax.ShapeDtypeStruct((tiles, LANES), F32),
        ),
        in_specs=[SMEM, VMEM, VMEM, VMEM, VMEM],
        out_specs=(VMEM, VMEM),
        compiler_params=pltpu.CompilerParams(vmem_limit_bytes=24 << 20),
        name="place",
    )(section, recv, total, area_far, sea)

    tail = lax.all_to_all(tail, "tile", 0, 0, tiled=True)

    out = pl.pallas_call(
        functools.partial(correct_kernel, fields=fields),
        out_shape=jax.ShapeDtypeStruct((1, fields, rows, cells), F32),
        in_specs=[SMEM, VMEM, VMEM, VMEM],
        out_specs=VMEM,
        compiler_params=pltpu.CompilerParams(vmem_limit_bytes=16 << 20),
        name="correct",
    )(section, masked, tail, sea)
    return lax.ppermute(out, "comp", swap)


def solution(mesh):
    placed = (
        P("comp", None, "tile", None),
        P("comp", "tile", None),
        P("tile", None),
        P("comp", "tile", None, None),
        P("comp", "tile"),
        P("comp", "tile", None),
        P("comp", "tile"),
    )
    return jax.shard_map(
        shards, mesh=mesh, in_specs=placed, out_specs=P("comp", None, "tile", None), check_vma=False
    )
```

time: 183 us -> 92.1 us (0.50)
  blocking collectives: 87.8 us -> 16.1 us
  matrix products: 31.9 us -> 0 us
  Pallas kernels: 0 us -> 19.5 us
  starting transfers between devices: 12.6 us -> 21.7 us
  waiting for transfers between devices: 39.1 us -> 30.1 us
  other arithmetic: 4.95 us -> 0 us
  local copies, waits for them, and re-layouts: 6.02 us -> 4.15 us
    psum x1 -> x0, blocking collectives: 66.3 us -> none  [shards(): source_total = lax.psum(source_terms, ('comp', 'tile'))]
    dot_general x3 -> x0, matrix products: 31.9 us -> none  [the longest x1 28.8 us: shards(): jnp.einsum('fkc,kdc->kfd', picked, weights[0], precision=lax.Precision.HI...]
    pallas_call x0 -> x4, Pallas kernels: none -> 19.5 us  [the longest x1 13.6 us: shards(): pl.pallas_call(functools.partial(products_kernel, blocks=blocks, fields=f...]
    ppermute x4, waiting for transfers between devices: 15.8 us -> 2.44 us  [the longest x1 1.54 us: shards(): return lax.ppermute(out, 'comp', swap)]
    all_to_all x1, starting transfers between devices: 5.01 us -> 12.4 us  [shards(): lax.all_to_all(packed.reshape(tiles, pitch, LANES), 'tile', 0, 0, tiled=T...]
    all_to_all x1, blocking collectives: 21.6 us -> 16.1 us  [shards(): tail = lax.all_to_all(tail, 'tile', 0, 0, tiled=True)]
    all_to_all x1, waiting for transfers between devices: 23.3 us -> 27.7 us  [shards(): lax.all_to_all(packed.reshape(tiles, pitch, LANES), 'tile', 0, 0, tiled=T...]
    unnamed x11 -> x15, local copies, waits for them, and re-layouts: 1.28 us -> 3.37 us
  transfers between devices with their start and end apart: 5 -> 5, of which waited for: 4 -> 3; matrix products, arithmetic and copies ran while one was open for 2% -> 0% of each run, Pallas kernels for 0% -> 15%
where the time goes in v1:
time: 92.1 us; the launch traced here: 91.6 us
  waiting for transfers between devices  30.1 us (33%)
  starting transfers between devices  21.7 us (24%)
  Pallas kernels  19.5 us (21%)
  blocking collectives  16.1 us (17%)
  local copies, waits for them, and re-layouts  4.15 us (5%)
    all_to_all x1, waiting for transfers between devices, shards(): lax.all_to_all(packed.reshape(tiles, pitch, LANES), 'tile', 0, 0, tiled=T...  27.7 us
    all_to_all x1, blocking collectives, shards(): tail = lax.all_to_all(tail, 'tile', 0, 0, tiled=True)  16.1 us
    pallas_call x1, Pallas kernels, shards(): pl.pallas_call(functools.partial(products_kernel, blocks=blocks, fields=f...  13.6 us
    all_to_all x1, starting transfers between devices, shards(): lax.all_to_all(packed.reshape(tiles, pitch, LANES), 'tile', 0, 0, tiled=T...  12.4 us
    pallas_call x1, Pallas kernels, shards(): pl.pallas_call(functools.partial(pack_kernel, blocks=blocks, fields=field...  4.56 us
    ppermute x1, starting transfers between devices, shards(): before = lax.ppermute(surface[0, :, rows - 1], 'tile', up)  4.36 us
    unnamed x15, local copies, waits for them, and re-layouts  3.37 us
    ppermute x1, starting transfers between devices, shards(): return lax.ppermute(out, 'comp', swap)  2.31 us
  transfers between devices with their start and end apart: 5, of which 3 were waited for; matrix products, arithmetic and copies ran while one was open for 0% of the time, Pallas kernels for 15%

profile of v1, /device:TPU:1, one launch (start us, length us, event | category | flops | bytes accessed | tf_op | source)
XLA Modules:
  0.0 91.6 jit_solution(14338864581496596254)
XLA Ops:
  0.0 0.8 fusion
  0.8 4.4 %collective-permute-start = (f32[8,128]{1,0:T(8,128)S(1)}, f32[8,128]{1,0:T(8,128)S(1)}, u32[]{:S(2)}, u32[]{:S(2)}) collective-permute-start(f32[8,128]{1,0:T(8,128)S(1)} %bitcast.18), channel_id=1, source_target_pairs={{0,1},{1,2},{2,3},{3,4},{4,5},{5,6},{6,7},{7,8},{8,9},{9,10},{10,1... | collective-permute-start | bytes 12296 | tf_op jit(solution)/shard_map/ppermute | solution.py:200
  5.1 1.3 %collective-permute-start.1 = (f32[8,128]{1,0:T(8,128)S(1)}, f32[8,128]{1,0:T(8,128)S(1)}, u32[]{:S(2)}, u32[]{:S(2)}) collective-permute-start(f32[8,128]{1,0:T(8,128)S(1)} %bitcast.17), channel_id=1, source_target_pairs={{1,0},{2,1},{3,2},{4,3},{5,4},{6,5},{7,6},{8,7},{9,8},{10,9},{11,1... | collective-permute-start | bytes 12296 | tf_op jit(solution)/shard_map/ppermute | solution.py:201
  6.4 0.0 copy-start
  6.5 1.0 %copy-done = f32[1,8,128,128]{3,2,1,0:T(8,128)S(1)} copy-done((f32[1,8,128,128]{3,2,1,0:T(8,128)S(1)}, f32[1,8,128,128]{3,2,1,0:T(8,128)}, u32[]{:S(2)}) %copy-start) | copy-done | bytes 524312
  7.5 0.0 copy-start.1
  7.5 0.8 copy-done.1
  8.3 0.0 copy-start.4
  8.3 0.7 copy-done.4
  9.0 0.0 copy-start.5
  9.0 0.0 copy-start.6
  9.0 13.6 %products.1 = (f32[2048,128]{1,0:T(8,128)S(1)}, f32[8,128]{1,0:T(8,128)S(1)}, f32[16,128,128]{2,1,0:T(8,128)}, s32[264]{0:T(512)S(1)}) custom-call(s32[1,256]{1,0:T(1,128)S(1)} %copy-done.4, f32[1,8,128,128]{3,2,1,0:T(8,128)S(1)} %copy-done, f32[1,128,128]{2,1,0:T(8,128)S(1)} %copy-done.1, f32[1,256,128,128]{3,2,1,0:T(8,128)} %w_ref.3), custom_call_target="tpu_custom_call" | custom-call | flops 200000000 | bytes 20971520 | tf_op jit(solution)/shard_map/products/pallas_call | solution.py:206
  22.7 0.0 collective-permute-done.before_ref
  22.7 0.0 collective-permute-done.1.after_ref
  22.7 0.0 copy-done.5
  22.7 0.0 copy-done.6
  22.7 4.6 %pack.1 = (f32[4608,128]{1,0:T(8,128)}, f32[8,128]{1,0:T(8,128)S(1)}) custom-call(s32[1,256]{1,0:T(1,128)S(1)} %copy-done.4, s32[256]{0:T(256)S(1)} %bitcast.15, s32[1,256]{1,0:T(1,128)S(1)} %copy-done.6, s32[264]{0:T(512)S(1)} %get-tuple-element.13.edge_ref, f32[2048,128]{1,0:T(8,128)S(1)} %get-tuple-element.14.prod_ref, ...), custom_call_target="tpu_custom_call" | custom-call | tf_op jit(solution)/shard_map/pack/pallas_call | solution.py:227
  27.3 0.0 copy-start.2
  27.3 0.0 copy-start.3
  27.3 12.4 %all-to-all-start = ((f32[64,72,128]{2,1,0:T(8,128)}), f32[64,72,128]{2,1,0:T(8,128)S(1)}, u32[]{:S(2)}, u32[]{:S(2)}) async-start(f32[64,72,128]{2,1,0:T(8,128)} %bitcast.16), calls=%async_computation | async-start | bytes 4718592 | tf_op jit(solution)/shard_map/all_to_all | solution.py:247
  39.7 0.0 copy-done.2
  39.7 1.3 %collective-permute-start.2 = (f32[1,128,128]{2,1,0:T(8,128)S(1)}, f32[1,128,128]{2,1,0:T(8,128)S(1)}, u32[]{:S(2)}, u32[]{:S(2)}) collective-permute-start(f32[1,128,128]{2,1,0:T(8,128)S(1)} %copy-done.2), channel_id=1, source_target_pairs={{0,64},{64,0},{1,65},{65,1},{2,66},{66,2},{3,67},{67,3},{4,68},{68... | collective-permute-start | bytes 196616 | tf_op jit(solution)/shard_map/ppermute | solution.py:202
  41.0 0.9 collective-permute-done.2.area_ref
  41.9 27.7 %all-to-all-done.recv_ref = f32[64,72,128]{2,1,0:T(8,128)S(1)} async-done(((f32[64,72,128]{2,1,0:T(8,128)}), f32[64,72,128]{2,1,0:T(8,128)S(1)}, u32[]{:S(2)}, u32[]{:S(2)}) %all-to-all-start) | async-done | bytes 2359328 | tf_op jit(solution)/shard_map/all_to_all | solution.py:247
  69.6 0.0 copy-done.3
  69.6 1.1 %place.1 = (f32[8,128,128]{2,1,0:T(8,128)S(1)}, f32[64,128]{1,0:T(8,128)S(1)}) custom-call(s32[1]{0:T(128)} %bitcast.section_ref, f32[64,72,128]{2,1,0:T(8,128)S(1)} %all-to-all-done.recv_ref, f32[8,128]{1,0:T(8,128)S(1)} %get-tuple-element.18.total_ref, f32[1,128,128]{2,1,0:T(8,128)S(1)} %collective-permute-done.2.area_ref, s32[128,128]{1,0:T(8,128)S(1)} %copy-done.3), custom_call_target="tpu_custom_call" | custom-call | tf_op jit(solution)/shard_map/place/pallas_call | solution.py:249
  70.7 16.1 %all_to_all.16 = f32[64,1,128]{2,1,0:T(1,128)S(1)} all-to-all(f32[64,1,128]{2,1,0:T(1,128)S(1)} %bitcast.14), channel_id=1, replica_groups=mesh['comp'=2,'tile'=64] {'tile'}, dimensions={0} | all-to-all | bytes 65536 | tf_op jit(solution)/shard_map/all_to_all | solution.py:261
  86.8 0.2 correct.1
  87.0 2.3 %collective-permute-start.3 = (f32[1,8,128,128]{3,2,1,0:T(8,128)S(1)}, f32[1,8,128,128]{3,2,1,0:T(8,128)S(1)}, u32[]{:S(2)}, u32[]{:S(2)}) collective-permute-start(f32[1,8,128,128]{3,2,1,0:T(8,128)S(1)} %correct.1), channel_id=1, source_target_pairs={{0,64},{64,0},{1,65},{65,1},{2,66},{66,2},{3,67},{67,3},{4,68},{68... | collective-permute-start | bytes 1572872 | tf_op jit(solution)/shard_map/ppermute | solution.py:271
  89.3 1.5 %collective-permute-done.3 = f32[1,8,128,128]{3,2,1,0:T(8,128)S(1)} collective-permute-done((f32[1,8,128,128]{3,2,1,0:T(8,128)S(1)}, f32[1,8,128,128]{3,2,1,0:T(8,128)S(1)}, u32[]{:S(2)}, u32[]{:S(2)}) %collective-permute-start.3) | collective-permute-done | bytes 524320 | tf_op jit(solution)/shard_map/ppermute | solution.py:271
  90.8 0.8 copy.16
Async XLA Ops:
  0.8 21.9 %collective-permute-start = (f32[8,128]{1,0:T(8,128)S(1)}, f32[8,128]{1,0:T(8,128)S(1)}, u32[]{:S(2)}, u32[]{:S(2)}) collective-permute-start(f32[8,128]{1,0:T(8,128)S(1)} %bitcast.18), channel_id=1, source_target_pairs={{0,1},{1,2},{2,3},{3,4},{4,5},{5,6},{6,7},{7,8},{8,9},{9,10},{10,1... | collective-permute-start | bytes 12296 | tf_op jit(solution)/shard_map/ppermute | solution.py:200
  5.1 17.5 %collective-permute-start.1 = (f32[8,128]{1,0:T(8,128)S(1)}, f32[8,128]{1,0:T(8,128)S(1)}, u32[]{:S(2)}, u32[]{:S(2)}) collective-permute-start(f32[8,128]{1,0:T(8,128)S(1)} %bitcast.17), channel_id=1, source_target_pairs={{1,0},{2,1},{3,2},{4,3},{5,4},{6,5},{7,6},{8,7},{9,8},{10,9},{11,1... | collective-permute-start | bytes 12296 | tf_op jit(solution)/shard_map/ppermute | solution.py:201
  6.4 1.0 %copy-start = (f32[1,8,128,128]{3,2,1,0:T(8,128)S(1)}, f32[1,8,128,128]{3,2,1,0:T(8,128)}, u32[]{:S(2)}) copy-start(f32[1,8,128,128]{3,2,1,0:T(8,128)} %surf_ref.1) | copy-start | bytes 1572868
  7.5 0.8 copy-start.1
  8.3 0.7 copy-start.4
  9.0 13.7 %copy-start.5 = (s32[1,256,1]{1,2,0:T(1,128)S(1)}, s32[1,256,1]{1,2,0:T(1,128)}, u32[]{:S(2)}) copy-start(s32[1,256,1]{1,2,0:T(1,128)} %param.12) | copy-start | bytes 3076
  9.0 13.7 %copy-start.6 = (s32[1,256]{1,0:T(1,128)S(1)}, s32[1,256]{1,0:T(1,128)}, u32[]{:S(2)}) copy-start(s32[1,256]{1,0:T(1,128)} %local_ref.1) | copy-start | bytes 3076
  27.3 12.4 %copy-start.2 = (f32[1,128,128]{2,1,0:T(8,128)S(1)}, f32[1,128,128]{2,1,0:T(8,128)}, u32[]{:S(2)}) copy-start(f32[1,128,128]{2,1,0:T(8,128)} %area_ref.3) | copy-start | bytes 196612
  27.3 42.3 %copy-start.3 = (s32[128,128]{1,0:T(8,128)S(1)}, s32[128,128]{1,0:T(8,128)}, u32[]{:S(2)}) copy-start(s32[128,128]{1,0:T(8,128)} %sea_ref.3) | copy-start | bytes 196612
  27.3 42.3 %all-to-all-start = ((f32[64,72,128]{2,1,0:T(8,128)}), f32[64,72,128]{2,1,0:T(8,128)S(1)}, u32[]{:S(2)}, u32[]{:S(2)}) async-start(f32[64,72,128]{2,1,0:T(8,128)} %bitcast.16), calls=%async_computation | async-start | bytes 4718592 | tf_op jit(solution)/shard_map/all_to_all | solution.py:247
  39.7 2.2 %collective-permute-start.2 = (f32[1,128,128]{2,1,0:T(8,128)S(1)}, f32[1,128,128]{2,1,0:T(8,128)S(1)}, u32[]{:S(2)}, u32[]{:S(2)}) collective-permute-start(f32[1,128,128]{2,1,0:T(8,128)S(1)} %copy-done.2), channel_id=1, source_target_pairs={{0,64},{64,0},{1,65},{65,1},{2,66},{66,2},{3,67},{67,3},{4,68},{68... | collective-permute-start | bytes 196616 | tf_op jit(solution)/shard_map/ppermute | solution.py:202
  87.0 3.9 %collective-permute-start.3 = (f32[1,8,128,128]{3,2,1,0:T(8,128)S(1)}, f32[1,8,128,128]{3,2,1,0:T(8,128)S(1)}, u32[]{:S(2)}, u32[]{:S(2)}) collective-permute-start(f32[1,8,128,128]{3,2,1,0:T(8,128)S(1)} %correct.1), channel_id=1, source_target_pairs={{0,64},{64,0},{1,65},{65,1},{2,66},{66,2},{3,67},{67,3},{4,68},{68... | collective-permute-start | bytes 1572872 | tf_op jit(solution)/shard_map/ppermute | solution.py:271

commit v2 on v1

v2 whole, which is shorter than its diff:
```python
import functools

import jax
import jax.numpy as jnp
from jax import lax
from jax.experimental import pallas as pl
from jax.experimental.pallas import tpu as pltpu
from jax.sharding import PartitionSpec as P

RATE = 0.2
LANES = 128
SUB = 8
CHUNKS = 8
PIECES = 4

F32 = jnp.float32
BF16 = jnp.bfloat16
I32 = jnp.int32


def split_rows(rows):
    lead = rows.astype(BF16).astype(F32)
    return jnp.concatenate([lead, rows - lead], axis=0).astype(BF16)


def block_product(rows2, w):
    lead = w.astype(BF16)
    rest = (w - lead.astype(F32)).astype(BF16)
    both = jnp.concatenate([lead, rest], axis=0)
    t = lax.dot_general(rows2, both, (((1,), (1,)), ((), ())), preferred_element_type=F32)
    t = t[:, :LANES] + t[:, LANES:]
    return t[:SUB] + t[SUB:]


def prepare_kernel(
    surf_ref, area_ref, smooth_ref, part_ref, rim_ref, *, fields, rows
):
    r_iota = lax.broadcasted_iota(I32, (rows, LANES), 0)
    c_iota = lax.broadcasted_iota(I32, (rows, LANES), 1)
    area = area_ref[0]
    rim_ref[0:1, :] = area[0:1]
    rim_ref[1:2, :] = area[rows - 1 : rows]
    for f in range(fields):
        s = surf_ref[0, f]
        n = jnp.where(r_iota > 0, pltpu.roll(s, 1, 0), 0.0)
        n += jnp.where(r_iota < rows - 1, pltpu.roll(s, rows - 1, 0), 0.0)
        n += jnp.where(c_iota > 0, pltpu.roll(s, 1, 1), 0.0)
        n += jnp.where(c_iota < LANES - 1, pltpu.roll(s, LANES - 1, 1), 0.0)
        sm = s + RATE * (n - 4.0 * s)
        part_ref[pl.ds(f, 1), :] = jnp.sum(area * sm, axis=0, keepdims=True)
        smooth_ref[pl.ds(f, rows, stride=fields), :] = sm


def products_kernel(
    section_ref, code_ref, smooth_ref, part_ref, rim_ref, before_ref, after_ref, far_ref, w_hbm,
    packed_ref, total_ref, area_ref,
    spot_ref, count, wbuf, rows2, w_sems,
    *, blocks, fields, rows, slots, tiles,
):
    per = blocks // CHUNKS
    pitch = (fields + 1) * slots

    def fetch(p):
        span = pl.ds(p * (per // PIECES), per // PIECES)
        return pltpu.make_async_copy(w_hbm.at[0, span], wbuf.at[span], w_sems.at[p])

    for p in range(CHUNKS * PIECES):
        fetch(p).start()

    area_ref[...] = far_ref[...]
    before = RATE * before_ref[...]
    after = RATE * after_ref[...]
    total_ref[...] = part_ref[...] + rim_ref[0:1] * before + rim_ref[1:2] * after

    def clear(t, carry):
        count[t] = 0
        base = pl.multiple_of(t * pitch + fields * slots, SUB)
        packed_ref[pl.ds(base, slots), :] = jnp.full((slots, LANES), -1.0, F32)
        return carry

    lax.fori_loop(0, tiles, clear, 0, unroll=8)

    def number(i, carry):
        codes = [code_ref[0, i * SUB + j] for j in range(SUB)]
        for j, code in enumerate(codes):
            t = code >> 14
            rank = count[t]
            count[t] = rank + 1
            at = t * pitch + rank
            spot_ref[i * SUB + j] = at * rows + (code & (rows - 1))
            local = jnp.full((1, LANES), (code >> 7) & (rows - 1), I32)
            packed_ref[pl.ds(at + fields * slots, 1), :] = local.astype(F32)
        return carry

    lax.fori_loop(0, blocks // SUB, number, 0)

    def halves(g, carry):
        rows2[g] = split_rows(smooth_ref[pl.ds(pl.multiple_of(g * SUB, SUB), SUB), :])
        return carry

    lax.fori_loop(0, rows, halves, 0, unroll=8)
    rows2[0] = split_rows(smooth_ref[0:SUB, :] + before)
    rows2[rows - 1] = split_rows(smooth_ref[pl.ds((rows - 1) * SUB, SUB), :] + after)

    def chunk(c, carry):
        spots = [spot_ref[c * per + b] for b in range(per)]
        for p in range(PIECES):
            fetch(c * PIECES + p).wait()
        for b, spot in enumerate(spots):
            out = block_product(rows2[spot & (rows - 1)], wbuf[c * per + b])
            packed_ref[pl.ds(spot >> 7, SUB, stride=slots), :] = out
        return carry

    lax.fori_loop(0, CHUNKS, chunk, 0)


def place_kernel(
    section_ref, recv_ref, total_ref, area_ref, sea_ref, masked_ref, tail_ref,
    *, fields, rows, slots, tiles,
):
    count = tiles * slots
    target = recv_ref[:, fields * slots :, :].reshape(count, LANES)
    lane = lax.broadcasted_iota(I32, (count, rows), 1).astype(F32)
    placing = jnp.where(target == lane, 1.0, 0.0).T.astype(BF16)
    used = target >= 0.0
    mask = jnp.where(section_ref[0] == 1, 1.0, sea_ref[...].astype(F32))
    weight = area_ref[0] * mask
    lane1 = lax.broadcasted_iota(I32, (1, LANES), 1)
    tail = jnp.where(lane1 == fields, jnp.sum(weight), 0.0)
    for f in range(fields):
        x = recv_ref[:, f * slots : (f + 1) * slots, :].reshape(count, LANES)
        x = jnp.where(used, x, 0.0)
        lead = x.astype(BF16)
        rest = (x - lead.astype(F32)).astype(BF16)
        got = jnp.dot(placing, lead, preferred_element_type=F32)
        got += jnp.dot(placing, rest, preferred_element_type=F32)
        masked_ref[f] = got * mask
        gap = jnp.sum(total_ref[pl.ds(f, 1), :]) - jnp.sum(weight * got)
        tail += jnp.where(lane1 == f, gap, 0.0)
    tail_ref[...] = jnp.broadcast_to(tail, (tiles, LANES))


def correct_kernel(section_ref, masked_ref, sums_ref, sea_ref, out_ref, *, fields):
    sums = sums_ref[...]
    lane1 = lax.broadcasted_iota(I32, (1, LANES), 1)
    whole = jnp.sum(jnp.where(lane1 == fields, sums, 0.0), axis=1, keepdims=True)
    deficit = sums / whole
    mask = jnp.where(section_ref[0] == 0, 1.0, sea_ref[...].astype(F32))
    for f in range(fields):
        d = jnp.sum(jnp.where(lane1 == f, deficit, 0.0), axis=1, keepdims=True)
        out_ref[0, f] = masked_ref[f] + mask * d


VMEM = pl.BlockSpec(memory_space=pltpu.VMEM)
SMEM = pl.BlockSpec(memory_space=pltpu.SMEM)
HBM = pl.BlockSpec(memory_space=pltpu.HBM)


def shards(surface, area, sea, weights, src_row, dst_tile, dst_local):
    tiles = lax.axis_size("tile")
    section = lax.axis_index("comp").astype(I32).reshape(1)
    _, fields, rows, cells = surface.shape
    blocks = weights.shape[1]
    slots = 2 * blocks // tiles
    pitch = (fields + 1) * slots
    swap = [(0, 1), (1, 0)]
    up = [(i, i + 1) for i in range(tiles - 1)]
    down = [(i + 1, i) for i in range(tiles - 1)]

    before = lax.ppermute(surface[0, :, rows - 1], "tile", up)
    after = lax.ppermute(surface[0, :, 0], "tile", down)
    area_far = lax.ppermute(area, "comp", swap)
    code = (dst_tile[:, :, 0] << 14) | (dst_local << 7) | src_row

    sizes = dict(blocks=blocks, fields=fields, rows=rows, slots=slots, tiles=tiles)
    smooth, part, rim = pl.pallas_call(
        functools.partial(prepare_kernel, fields=fields, rows=rows),
        out_shape=(
            jax.ShapeDtypeStruct((rows * fields, LANES), F32),
            jax.ShapeDtypeStruct((fields, LANES), F32),
            jax.ShapeDtypeStruct((SUB, LANES), F32),
        ),
        in_specs=[VMEM, VMEM],
        out_specs=(VMEM, VMEM, VMEM),
        compiler_params=pltpu.CompilerParams(vmem_limit_bytes=8 << 20),
        cost_estimate=pl.CostEstimate(flops=10**7, bytes_accessed=8 << 20, transcendentals=0),
        name="prepare",
    )(surface, area)

    packed, total, area_far = pl.pallas_call(
        functools.partial(products_kernel, **sizes),
        out_shape=(
            jax.ShapeDtypeStruct((tiles * pitch, LANES), F32),
            jax.ShapeDtypeStruct((fields, LANES), F32),
            jax.ShapeDtypeStruct((1, rows, cells), F32),
        ),
        in_specs=[SMEM] * 2 + [VMEM] * 6 + [HBM],
        out_specs=(VMEM, VMEM, VMEM),
        scratch_shapes=[
            pltpu.SMEM((blocks,), I32),
            pltpu.SMEM((tiles,), I32),
            pltpu.VMEM((blocks, cells, cells), F32),
            pltpu.VMEM((rows, 2 * SUB, cells), BF16),
            pltpu.SemaphoreType.DMA((CHUNKS * PIECES,)),
        ],
        compiler_params=pltpu.CompilerParams(vmem_limit_bytes=46 << 20),
        cost_estimate=pl.CostEstimate(flops=2 * 10**8, bytes_accessed=20 << 20, transcendentals=0),
        name="products",
    )(section, code, smooth, part, rim, before, after, area_far, weights)

    recv = lax.all_to_all(packed.reshape(tiles, pitch, LANES), "tile", 0, 0, tiled=True)

    masked, tail = pl.pallas_call(
        functools.partial(place_kernel, fields=fields, rows=rows, slots=slots, tiles=tiles),
        out_shape=(
            jax.ShapeDtypeStruct((fields, rows, cells), F32),
            jax.ShapeDtypeStruct((tiles, LANES), F32),
        ),
        in_specs=[SMEM, VMEM, VMEM, VMEM, VMEM],
        out_specs=(VMEM, VMEM),
        compiler_params=pltpu.CompilerParams(vmem_limit_bytes=24 << 20),
        name="place",
    )(section, recv, total, area_far, sea)

    masked = lax.ppermute(masked, "comp", swap)
    tail = lax.all_to_all(tail, "tile", 0, 0, tiled=True)
    sums = lax.ppermute(jnp.sum(tail, axis=0, keepdims=True), "comp", swap)

    return pl.pallas_call(
        functools.partial(correct_kernel, fields=fields),
        out_shape=jax.ShapeDtypeStruct((1, fields, rows, cells), F32),
        in_specs=[SMEM, VMEM, VMEM, VMEM],
        out_specs=VMEM,
        compiler_params=pltpu.CompilerParams(vmem_limit_bytes=16 << 20),
        name="correct",
    )(section, masked, sums, sea)


def solution(mesh):
    placed = (
        P("comp", None, "tile", None),
        P("comp", "tile", None),
        P("tile", None),
        P("comp", "tile", None, None),
        P("comp", "tile"),
        P("comp", "tile", None),
        P("comp", "tile"),
    )
    return jax.shard_map(
        shards, mesh=mesh, in_specs=placed, out_specs=P("comp", None, "tile", None), check_vma=False
    )
```

time: 92.1 us -> 83 us (0.901)
  blocking collectives: 16.1 us -> 56.2 us
  waiting for transfers between devices: 30.1 us -> 0.83 us
  starting transfers between devices: 21.7 us -> 11.5 us
  Pallas kernels: 19.5 us -> 10.5 us
  local copies, waits for them, and re-layouts: 4.15 us -> 2.67 us
    all_to_all x0 -> x1, blocking collectives: none -> 43.1 us  [shards(): lax.all_to_all(packed.reshape(tiles, pitch, LANES), 'tile', 0, 0, tiled=T...]
    all_to_all x1 -> x0, waiting for transfers between devices: 27.7 us -> none  [shards(): lax.all_to_all(packed.reshape(tiles, pitch, LANES), 'tile', 0, 0, tiled=T...]
    all_to_all x1 -> x0, starting transfers between devices: 12.4 us -> none  [shards(): lax.all_to_all(packed.reshape(tiles, pitch, LANES), 'tile', 0, 0, tiled=T...]
    pallas_call x2, Pallas kernels: 18.2 us -> 8.38 us  [the longest x1 7.99 us: shards(): pl.pallas_call(functools.partial(products_kernel, **sizes), out_shape=(ja...]
    all_to_all x1, blocking collectives: 16.1 us -> 13.2 us  [shards(): tail = lax.all_to_all(tail, 'tile', 0, 0, tiled=True)]
    ppermute x1 -> x2, starting transfers between devices: 2.31 us -> 4.85 us  [the longest x1 3.32 us: shards(): masked = lax.ppermute(masked, 'comp', swap)]
    unnamed x15 -> x6, local copies, waits for them, and re-layouts: 3.37 us -> 1.89 us
  transfers between devices with their start and end apart: 5 -> 5, of which waited for: 3 -> 1; matrix products, arithmetic and copies ran while one was open for 0% -> 1% of each run, Pallas kernels for 15% -> 0%
where the time goes in v2:
time: 83 us; the launch traced here: 82.6 us
  blocking collectives  56.2 us (68%)
  starting transfers between devices  11.5 us (14%)
  Pallas kernels  10.5 us (13%)
  local copies, waits for them, and re-layouts  2.67 us (3%)
    all_to_all x1, blocking collectives, shards(): lax.all_to_all(packed.reshape(tiles, pitch, LANES), 'tile', 0, 0, tiled=T...  43.1 us
    all_to_all x1, blocking collectives, shards(): tail = lax.all_to_all(tail, 'tile', 0, 0, tiled=True)  13.2 us
    pallas_call x1, Pallas kernels, shards(): pl.pallas_call(functools.partial(products_kernel, **sizes), out_shape=(ja...  7.99 us
    ppermute x1, starting transfers between devices, shards(): before = lax.ppermute(surface[0, :, rows - 1], 'tile', up)  4.36 us
    ppermute x1, starting transfers between devices, shards(): masked = lax.ppermute(masked, 'comp', swap)  3.32 us
    unnamed x6, local copies, waits for them, and re-layouts  1.89 us
  transfers between devices with their start and end apart: 5, of which 1 were waited for; matrix products, arithmetic and copies ran while one was open for 1% of the time, Pallas kernels for 0%

profile of v2, /device:TPU:1, one launch (start us, length us, event | category | flops | bytes accessed | tf_op | source)
XLA Modules:
  0.0 82.6 jit_solution(10532591992335087510)
XLA Ops:
  0.0 0.8 fusion.1
  0.8 4.4 %collective-permute-start = (f32[8,128]{1,0:T(8,128)S(1)}, f32[8,128]{1,0:T(8,128)S(1)}, u32[]{:S(2)}, u32[]{:S(2)}) collective-permute-start(f32[8,128]{1,0:T(8,128)S(1)} %bitcast.19), channel_id=1, source_target_pairs={{0,1},{1,2},{2,3},{3,4},{4,5},{5,6},{6,7},{7,8},{8,9},{9,10},{10,1... | collective-permute-start | bytes 12296 | tf_op jit(solution)/shard_map/ppermute | solution.py:170
  5.1 1.3 %collective-permute-start.1 = (f32[8,128]{1,0:T(8,128)S(1)}, f32[8,128]{1,0:T(8,128)S(1)}, u32[]{:S(2)}, u32[]{:S(2)}) collective-permute-start(f32[8,128]{1,0:T(8,128)S(1)} %bitcast.18), channel_id=1, source_target_pairs={{1,0},{2,1},{3,2},{4,3},{5,4},{6,5},{7,6},{8,7},{9,8},{10,9},{11,1... | collective-permute-start | bytes 12296 | tf_op jit(solution)/shard_map/ppermute | solution.py:171
  6.4 1.0 %collective-permute-start.2 = (f32[1,128,128]{2,1,0:T(8,128)}, f32[1,128,128]{2,1,0:T(8,128)S(1)}, u32[]{:S(2)}, u32[]{:S(2)}) collective-permute-start(f32[1,128,128]{2,1,0:T(8,128)} %area_ref.1), channel_id=1, source_target_pairs={{0,64},{64,0},{1,65},{65,1},{2,66},{66,2},{3,67},{67,3},{4,68},{68... | collective-permute-start | bytes 196616 | tf_op jit(solution)/shard_map/ppermute | solution.py:172
  7.5 0.7 fusion.code_ref
  8.2 0.0 copy-start
  8.2 1.0 %copy-done = f32[1,8,128,128]{3,2,1,0:T(8,128)S(1)} copy-done((f32[1,8,128,128]{3,2,1,0:T(8,128)S(1)}, f32[1,8,128,128]{3,2,1,0:T(8,128)}, u32[]{:S(2)}) %copy-start) | copy-done | bytes 524312
  9.2 0.0 copy-start.2
  9.2 0.8 %copy-done.2 = f32[1,128,128]{2,1,0:T(8,128)S(1)} copy-done((f32[1,128,128]{2,1,0:T(8,128)S(1)}, f32[1,128,128]{2,1,0:T(8,128)}, u32[]{:S(2)}) %copy-start.2) | copy-done | bytes 65560
  10.1 0.4 prepare.1
  10.5 0.0 collective-permute-done.before_ref
  10.5 0.0 collective-permute-done.1.after_ref
  10.5 0.0 collective-permute-done.2.far_ref
  10.5 8.0 %products.1 = (f32[4608,128]{1,0:T(8,128)S(1)}, f32[8,128]{1,0:T(8,128)S(1)}, f32[1,128,128]{2,1,0:T(8,128)S(1)}) custom-call(s32[1]{0:T(128)} %bitcast.section_ref, s32[1,256]{1,0:T(1,128)S(1)} %fusion.code_ref, f32[1024,128]{1,0:T(8,128)S(1)} %get-tuple-element.13.smooth_ref, f32[8,128]{1,0:T(8,128)S(1)} %get-tuple-element.14.part_ref, ...), custom_call_target="tpu_custom_call" | custom-call | flops 200000000 | bytes 20971520 | tf_op jit(solution)/shard_map/products/pallas_call | solution.py:190
  18.5 0.0 copy-start.1
  18.5 43.1 %all_to_all.14.recv_ref = f32[64,72,128]{2,1,0:T(8,128)S(1)} all-to-all(f32[64,72,128]{2,1,0:T(8,128)S(1)} %bitcast.16), channel_id=1, replica_groups=mesh['comp'=2,'tile'=64] {'tile'}, dimensions={0} | all-to-all | bytes 4718592 | tf_op jit(solution)/shard_map/all_to_all | solution.py:211
  61.6 0.0 copy-done.1
  61.6 1.1 %place.1 = (f32[8,128,128]{2,1,0:T(8,128)S(1)}, f32[64,128]{1,0:T(8,128)S(1)}) custom-call(s32[1]{0:T(128)} %bitcast.section_ref, f32[64,72,128]{2,1,0:T(8,128)S(1)} %all_to_all.14.recv_ref, f32[8,128]{1,0:T(8,128)S(1)} %get-tuple-element.17.total_ref, f32[1,128,128]{2,1,0:T(8,128)S(1)} %get-tuple-element.18.area_ref, s32[128,128]{1,0:T(8,128)S(1)} %copy-done.1), custom_call_target="tpu_custom_call" | custom-call | tf_op jit(solution)/shard_map/place/pallas_call | solution.py:213
  62.7 3.3 %collective-permute-start.3 = (f32[8,128,128]{2,1,0:T(8,128)S(1)}, f32[8,128,128]{2,1,0:T(8,128)S(1)}, u32[]{:S(2)}, u32[]{:S(2)}) collective-permute-start(f32[8,128,128]{2,1,0:T(8,128)S(1)} %get-tuple-element.19), channel_id=1, source_target_pairs={{0,64},{64,0},{1,65},{65,1},{2,66},{66,2},{3,67},{67,3},{4,68},{68... | collective-permute-start | bytes 1572872 | tf_op jit(solution)/shard_map/ppermute | solution.py:225
  66.0 13.2 %all_to_all.15 = f32[64,1,128]{2,1,0:T(1,128)S(1)} all-to-all(f32[64,1,128]{2,1,0:T(1,128)S(1)} %bitcast.17), channel_id=1, replica_groups=mesh['comp'=2,'tile'=64] {'tile'}, dimensions={0} | all-to-all | bytes 65536 | tf_op jit(solution)/shard_map/all_to_all | solution.py:226
  79.2 0.1 reduce_sum.9
  79.3 1.5 %collective-permute-start.4 = (f32[1,128]{1,0:T(1,128)S(1)}, f32[1,128]{1,0:T(1,128)S(1)}, u32[]{:S(2)}, u32[]{:S(2)}) collective-permute-start(f32[1,128]{1,0:T(1,128)S(1)} %bitcast.20), channel_id=1, source_target_pairs={{0,64},{64,0},{1,65},{65,1},{2,66},{66,2},{3,67},{67,3},{4,68},{68... | collective-permute-start | bytes 1544 | tf_op jit(solution)/shard_map/ppermute | solution.py:227
  80.8 0.8 collective-permute-done.4.sums_ref
  81.6 0.0 collective-permute-done.3.masked_ref
  81.6 1.0 %correct.1 = f32[1,8,128,128]{3,2,1,0:T(8,128)} custom-call(s32[1]{0:T(128)} %bitcast.section_ref, f32[8,128,128]{2,1,0:T(8,128)S(1)} %collective-permute-done.3.masked_ref, f32[1,128]{1,0:T(1,128)S(1)} %collective-permute-done.4.sums_ref, s32[128,128]{1,0:T(8,128)S(1)} %copy-done.1), custom_call_target="tpu_custom_call" | custom-call | tf_op jit(solution)/shard_map/correct/pallas_call | solution.py:229
Async XLA Ops:
  0.8 9.7 %collective-permute-start = (f32[8,128]{1,0:T(8,128)S(1)}, f32[8,128]{1,0:T(8,128)S(1)}, u32[]{:S(2)}, u32[]{:S(2)}) collective-permute-start(f32[8,128]{1,0:T(8,128)S(1)} %bitcast.19), channel_id=1, source_target_pairs={{0,1},{1,2},{2,3},{3,4},{4,5},{5,6},{6,7},{7,8},{8,9},{9,10},{10,1... | collective-permute-start | bytes 12296 | tf_op jit(solution)/shard_map/ppermute | solution.py:170
  5.1 5.3 %collective-permute-start.1 = (f32[8,128]{1,0:T(8,128)S(1)}, f32[8,128]{1,0:T(8,128)S(1)}, u32[]{:S(2)}, u32[]{:S(2)}) collective-permute-start(f32[8,128]{1,0:T(8,128)S(1)} %bitcast.18), channel_id=1, source_target_pairs={{1,0},{2,1},{3,2},{4,3},{5,4},{6,5},{7,6},{8,7},{9,8},{10,9},{11,1... | collective-permute-start | bytes 12296 | tf_op jit(solution)/shard_map/ppermute | solution.py:171
  6.4 4.0 %collective-permute-start.2 = (f32[1,128,128]{2,1,0:T(8,128)}, f32[1,128,128]{2,1,0:T(8,128)S(1)}, u32[]{:S(2)}, u32[]{:S(2)}) collective-permute-start(f32[1,128,128]{2,1,0:T(8,128)} %area_ref.1), channel_id=1, source_target_pairs={{0,64},{64,0},{1,65},{65,1},{2,66},{66,2},{3,67},{67,3},{4,68},{68... | collective-permute-start | bytes 196616 | tf_op jit(solution)/shard_map/ppermute | solution.py:172
  8.2 1.0 %copy-start = (f32[1,8,128,128]{3,2,1,0:T(8,128)S(1)}, f32[1,8,128,128]{3,2,1,0:T(8,128)}, u32[]{:S(2)}) copy-start(f32[1,8,128,128]{3,2,1,0:T(8,128)} %surf_ref.1) | copy-start | bytes 1572868
  9.2 0.8 %copy-start.2 = (f32[1,128,128]{2,1,0:T(8,128)S(1)}, f32[1,128,128]{2,1,0:T(8,128)}, u32[]{:S(2)}) copy-start(f32[1,128,128]{2,1,0:T(8,128)} %area_ref.1) | copy-start | bytes 196612
  18.5 43.1 %copy-start.1 = (s32[128,128]{1,0:T(8,128)S(1)}, s32[128,128]{1,0:T(8,128)}, u32[]{:S(2)}) copy-start(s32[128,128]{1,0:T(8,128)} %sea_ref.3) | copy-start | bytes 196612
  62.7 18.9 %collective-permute-start.3 = (f32[8,128,128]{2,1,0:T(8,128)S(1)}, f32[8,128,128]{2,1,0:T(8,128)S(1)}, u32[]{:S(2)}, u32[]{:S(2)}) collective-permute-start(f32[8,128,128]{2,1,0:T(8,128)S(1)} %get-tuple-element.19), channel_id=1, source_target_pairs={{0,64},{64,0},{1,65},{65,1},{2,66},{66,2},{3,67},{67,3},{4,68},{68... | collective-permute-start | bytes 1572872 | tf_op jit(solution)/shard_map/ppermute | solution.py:225
  79.3 2.3 %collective-permute-start.4 = (f32[1,128]{1,0:T(1,128)S(1)}, f32[1,128]{1,0:T(1,128)S(1)}, u32[]{:S(2)}, u32[]{:S(2)}) collective-permute-start(f32[1,128]{1,0:T(1,128)S(1)} %bitcast.20), channel_id=1, source_target_pairs={{0,64},{64,0},{1,65},{65,1},{2,66},{66,2},{3,67},{67,3},{4,68},{68... | collective-permute-start | bytes 1544 | tf_op jit(solution)/shard_map/ppermute | solution.py:227

commit v3 on v2

--- a/solution.py
+++ b/solution.py
@@ -11,7 +11,7 @@
 LANES = 128
 SUB = 8
 CHUNKS = 8
-PIECES = 4
+PIECES = 2
 
 F32 = jnp.float32
 BF16 = jnp.bfloat16
@@ -54,11 +54,11 @@
 def products_kernel(
     section_ref, code_ref, smooth_ref, part_ref, rim_ref, before_ref, after_ref, far_ref, w_hbm,
     packed_ref, total_ref, area_ref,
-    spot_ref, count, wbuf, rows2, w_sems,
+    spot_ref, count, index, wbuf, rows2, w_sems,
     *, blocks, fields, rows, slots, tiles,
 ):
     per = blocks // CHUNKS
-    pitch = (fields + 1) * slots
+    pitch = fields * slots + 1
 
     def fetch(p):
         span = pl.ds(p * (per // PIECES), per // PIECES)
@@ -74,11 +74,10 @@
 
     def clear(t, carry):
         count[t] = 0
-        base = pl.multiple_of(t * pitch + fields * slots, SUB)
-        packed_ref[pl.ds(base, slots), :] = jnp.full((slots, LANES), -1.0, F32)
         return carry
 
     lax.fori_loop(0, tiles, clear, 0, unroll=8)
+    index[...] = jnp.full((tiles * slots, LANES), -1.0, F32)
 
     def number(i, carry):
         codes = [code_ref[0, i * SUB + j] for j in range(SUB)]
@@ -86,13 +85,16 @@
             t = code >> 14
             rank = count[t]
             count[t] = rank + 1
-            at = t * pitch + rank
-            spot_ref[i * SUB + j] = at * rows + (code & (rows - 1))
+            spot_ref[i * SUB + j] = (t * pitch + rank) * rows + (code & (rows - 1))
             local = jnp.full((1, LANES), (code >> 7) & (rows - 1), I32)
-            packed_ref[pl.ds(at + fields * slots, 1), :] = local.astype(F32)
+            index[pl.ds(t * slots + rank, 1), :] = local.astype(F32)
         return carry
 
     lax.fori_loop(0, blocks // SUB, number, 0)
+    slot = lax.broadcasted_iota(I32, (tiles, slots, LANES), 1)
+    lane = lax.broadcasted_iota(I32, (tiles, slots, LANES), 2)
+    own = jnp.where(slot == lane, index[...].reshape(tiles, slots, LANES), 0.0)
+    packed_ref[pl.ds(fields * slots, tiles, stride=pitch), :] = jnp.sum(own, axis=1)
 
     def halves(g, carry):
         rows2[g] = split_rows(smooth_ref[pl.ds(pl.multiple_of(g * SUB, SUB), SUB), :])
@@ -118,17 +120,22 @@
     section_ref, recv_ref, total_ref, area_ref, sea_ref, masked_ref, tail_ref,
     *, fields, rows, slots, tiles,
 ):
-    count = tiles * slots
-    target = recv_ref[:, fields * slots :, :].reshape(count, LANES)
-    lane = lax.broadcasted_iota(I32, (count, rows), 1).astype(F32)
-    placing = jnp.where(target == lane, 1.0, 0.0).T.astype(BF16)
+    pitch = fields * slots + 1
+    targets = recv_ref[pl.ds(fields * slots, tiles, stride=pitch), :]
+    lane = lax.broadcasted_iota(I32, (tiles, rows), 1).astype(F32)
+    target = jnp.concatenate(
+        [jnp.broadcast_to(targets[:, j : j + 1], (tiles, rows)) for j in range(slots)], axis=0
+    )
+    placing = jnp.where(target == jnp.concatenate([lane] * slots, axis=0), 1.0, 0.0).T.astype(BF16)
     used = target >= 0.0
     mask = jnp.where(section_ref[0] == 1, 1.0, sea_ref[...].astype(F32))
     weight = area_ref[0] * mask
     lane1 = lax.broadcasted_iota(I32, (1, LANES), 1)
     tail = jnp.where(lane1 == fields, jnp.sum(weight), 0.0)
     for f in range(fields):
-        x = recv_ref[:, f * slots : (f + 1) * slots, :].reshape(count, LANES)
+        x = jnp.concatenate(
+            [recv_ref[pl.ds(f * slots + j, tiles, stride=pitch), :] for j in range(slots)], axis=0
+        )
         x = jnp.where(used, x, 0.0)
         lead = x.astype(BF16)
         rest = (x - lead.astype(F32)).astype(BF16)
@@ -162,7 +169,7 @@
     _, fields, rows, cells = surface.shape
     blocks = weights.shape[1]
     slots = 2 * blocks // tiles
-    pitch = (fields + 1) * slots
+    pitch = fields * slots + 1
     swap = [(0, 1), (1, 0)]
     up = [(i, i + 1) for i in range(tiles - 1)]
     down = [(i + 1, i) for i in range(tiles - 1)]
@@ -199,6 +206,7 @@
         scratch_shapes=[
             pltpu.SMEM((blocks,), I32),
             pltpu.SMEM((tiles,), I32),
+            pltpu.VMEM((tiles * slots, LANES), F32),
             pltpu.VMEM((blocks, cells, cells), F32),
             pltpu.VMEM((rows, 2 * SUB, cells), BF16),
             pltpu.SemaphoreType.DMA((CHUNKS * PIECES,)),
@@ -208,7 +216,8 @@
         name="products",
     )(section, code, smooth, part, rim, before, after, area_far, weights)
 
-    recv = lax.all_to_all(packed.reshape(tiles, pitch, LANES), "tile", 0, 0, tiled=True)
+    flat = packed.reshape(tiles, 1, pitch * LANES)
+    recv = lax.all_to_all(flat, "tile", 0, 0, tiled=True).reshape(tiles * pitch, LANES)
 
     masked, tail = pl.pallas_call(
         functools.partial(place_kernel, fields=fields, rows=rows, slots=slots, tiles=tiles),

time: 83 us -> 80.9 us (0.975)
  blocking collectives: 56.2 us -> 53.8 us
    all_to_all x1, blocking collectives: 43.1 us -> 40.8 us  [shards(): lax.all_to_all(flat, 'tile', 0, 0, tiled=True).reshape(tiles * pitch, LANES)]
where the time goes in v3:
time: 80.9 us; the launch traced here: 80.4 us
  blocking collectives  53.8 us (67%)
  starting transfers between devices  11.6 us (14%)
  Pallas kernels  10.6 us (13%)
  local copies, waits for them, and re-layouts  2.67 us (3%)
  waiting for transfers between devices  0.83 us (1%)
    all_to_all x1, blocking collectives, shards(): lax.all_to_all(flat, 'tile', 0, 0, tiled=True).reshape(tiles * pitch, LANES)  40.8 us
    all_to_all x1, blocking collectives, shards(): tail = lax.all_to_all(tail, 'tile', 0, 0, tiled=True)  13.1 us
    pallas_call x1, Pallas kernels, shards(): pl.pallas_call(functools.partial(products_kernel, **sizes), out_shape=(ja...  7.95 us
    ppermute x1, starting transfers between devices, shards(): before = lax.ppermute(surface[0, :, rows - 1], 'tile', up)  4.36 us
    ppermute x1, starting transfers between devices, shards(): masked = lax.ppermute(masked, 'comp', swap)  3.42 us
    unnamed x6, local copies, waits for them, and re-layouts  1.89 us
  transfers between devices with their start and end apart: 5, of which 1 were waited for; matrix products, arithmetic and copies ran while one was open for 1% of the time, Pallas kernels for 0%

profile of v3, /device:TPU:1, one launch (start us, length us, event | category | flops | bytes accessed | tf_op | source)
XLA Modules:
  0.0 80.4 jit_solution(9256389091066371332)
XLA Ops:
  0.0 0.8 fusion.1
  0.8 4.4 %collective-permute-start = (f32[8,128]{1,0:T(8,128)S(1)}, f32[8,128]{1,0:T(8,128)S(1)}, u32[]{:S(2)}, u32[]{:S(2)}) collective-permute-start(f32[8,128]{1,0:T(8,128)S(1)} %bitcast.21), channel_id=1, source_target_pairs={{0,1},{1,2},{2,3},{3,4},{4,5},{5,6},{6,7},{7,8},{8,9},{9,10},{10,1... | collective-permute-start | bytes 12296 | tf_op jit(solution)/shard_map/ppermute | solution.py:177
  5.1 1.3 %collective-permute-start.1 = (f32[8,128]{1,0:T(8,128)S(1)}, f32[8,128]{1,0:T(8,128)S(1)}, u32[]{:S(2)}, u32[]{:S(2)}) collective-permute-start(f32[8,128]{1,0:T(8,128)S(1)} %bitcast.20), channel_id=1, source_target_pairs={{1,0},{2,1},{3,2},{4,3},{5,4},{6,5},{7,6},{8,7},{9,8},{10,9},{11,1... | collective-permute-start | bytes 12296 | tf_op jit(solution)/shard_map/ppermute | solution.py:178
  6.4 1.0 %collective-permute-start.2 = (f32[1,128,128]{2,1,0:T(8,128)}, f32[1,128,128]{2,1,0:T(8,128)S(1)}, u32[]{:S(2)}, u32[]{:S(2)}) collective-permute-start(f32[1,128,128]{2,1,0:T(8,128)} %area_ref.1), channel_id=1, source_target_pairs={{0,64},{64,0},{1,65},{65,1},{2,66},{66,2},{3,67},{67,3},{4,68},{68... | collective-permute-start | bytes 196616 | tf_op jit(solution)/shard_map/ppermute | solution.py:179
  7.5 0.7 fusion.code_ref
  8.2 0.0 copy-start
  8.2 1.0 %copy-done = f32[1,8,128,128]{3,2,1,0:T(8,128)S(1)} copy-done((f32[1,8,128,128]{3,2,1,0:T(8,128)S(1)}, f32[1,8,128,128]{3,2,1,0:T(8,128)}, u32[]{:S(2)}) %copy-start) | copy-done | bytes 524312
  9.2 0.0 copy-start.2
  9.2 0.8 %copy-done.2 = f32[1,128,128]{2,1,0:T(8,128)S(1)} copy-done((f32[1,128,128]{2,1,0:T(8,128)S(1)}, f32[1,128,128]{2,1,0:T(8,128)}, u32[]{:S(2)}) %copy-start.2) | copy-done | bytes 65560
  10.1 0.4 prepare.1
  10.5 0.0 collective-permute-done.before_ref
  10.5 0.0 collective-permute-done.1.after_ref
  10.5 0.0 collective-permute-done.2.far_ref
  10.5 8.0 %products.1 = (f32[4160,128]{1,0:T(8,128)S(1)}, f32[8,128]{1,0:T(8,128)S(1)}, f32[1,128,128]{2,1,0:T(8,128)S(1)}) custom-call(s32[1]{0:T(128)} %bitcast.section_ref, s32[1,256]{1,0:T(1,128)S(1)} %fusion.code_ref, f32[1024,128]{1,0:T(8,128)S(1)} %get-tuple-element.13.smooth_ref, f32[8,128]{1,0:T(8,128)S(1)} %get-tuple-element.14.part_ref, ...), custom_call_target="tpu_custom_call" | custom-call | flops 200000000 | bytes 20971520 | tf_op jit(solution)/shard_map/products/pallas_call | solution.py:197
  18.5 0.0 copy-start.1
  18.5 40.8 %all_to_all.14 = f32[64,1,8320]{2,1,0:T(1,128)S(1)} all-to-all(f32[64,1,8320]{2,1,0:T(1,128)S(1)} %bitcast.18), channel_id=1, replica_groups=mesh['comp'=2,'tile'=64] {'tile'}, dimensions={0} | all-to-all | bytes 4259840 | tf_op jit(solution)/shard_map/all_to_all | solution.py:220
  59.3 0.0 copy-done.1
  59.3 1.3 %place.1 = (f32[8,128,128]{2,1,0:T(8,128)S(1)}, f32[64,128]{1,0:T(8,128)S(1)}) custom-call(s32[1]{0:T(128)} %bitcast.section_ref, f32[4160,128]{1,0:T(8,128)S(1)} %bitcast.17, f32[8,128]{1,0:T(8,128)S(1)} %get-tuple-element.17.total_ref, f32[1,128,128]{2,1,0:T(8,128)S(1)} %get-tuple-element.18.area_ref, s32[128,128]{1,0:T(8,128)S(1)} %copy-done.1), custom_call_target="tpu_custom_call" | custom-call | tf_op jit(solution)/shard_map/place/pallas_call | solution.py:222
  60.5 3.4 %collective-permute-start.3 = (f32[8,128,128]{2,1,0:T(8,128)S(1)}, f32[8,128,128]{2,1,0:T(8,128)S(1)}, u32[]{:S(2)}, u32[]{:S(2)}) collective-permute-start(f32[8,128,128]{2,1,0:T(8,128)S(1)} %get-tuple-element.19), channel_id=1, source_target_pairs={{0,64},{64,0},{1,65},{65,1},{2,66},{66,2},{3,67},{67,3},{4,68},{68... | collective-permute-start | bytes 1572872 | tf_op jit(solution)/shard_map/ppermute | solution.py:234
  63.9 13.1 %all_to_all.15 = f32[64,1,128]{2,1,0:T(1,128)S(1)} all-to-all(f32[64,1,128]{2,1,0:T(1,128)S(1)} %bitcast.19), channel_id=1, replica_groups=mesh['comp'=2,'tile'=64] {'tile'}, dimensions={0} | all-to-all | bytes 65536 | tf_op jit(solution)/shard_map/all_to_all | solution.py:235
  77.0 0.1 reduce_sum.9
  77.1 1.5 %collective-permute-start.4 = (f32[1,128]{1,0:T(1,128)S(1)}, f32[1,128]{1,0:T(1,128)S(1)}, u32[]{:S(2)}, u32[]{:S(2)}) collective-permute-start(f32[1,128]{1,0:T(1,128)S(1)} %bitcast.22), channel_id=1, source_target_pairs={{0,64},{64,0},{1,65},{65,1},{2,66},{66,2},{3,67},{67,3},{4,68},{68... | collective-permute-start | bytes 1544 | tf_op jit(solution)/shard_map/ppermute | solution.py:236
  78.6 0.8 %collective-permute-done.4.sums_ref = f32[1,128]{1,0:T(1,128)S(1)} collective-permute-done((f32[1,128]{1,0:T(1,128)S(1)}, f32[1,128]{1,0:T(1,128)S(1)}, u32[]{:S(2)}, u32[]{:S(2)}) %collective-permute-start.4) | collective-permute-done | bytes 544 | tf_op jit(solution)/shard_map/ppermute | solution.py:236
  79.4 0.0 collective-permute-done.3.masked_ref
  79.4 1.0 %correct.1 = f32[1,8,128,128]{3,2,1,0:T(8,128)} custom-call(s32[1]{0:T(128)} %bitcast.section_ref, f32[8,128,128]{2,1,0:T(8,128)S(1)} %collective-permute-done.3.masked_ref, f32[1,128]{1,0:T(1,128)S(1)} %collective-permute-done.4.sums_ref, s32[128,128]{1,0:T(8,128)S(1)} %copy-done.1), custom_call_target="tpu_custom_call" | custom-call | tf_op jit(solution)/shard_map/correct/pallas_call | solution.py:238
Async XLA Ops:
  0.8 9.7 %collective-permute-start = (f32[8,128]{1,0:T(8,128)S(1)}, f32[8,128]{1,0:T(8,128)S(1)}, u32[]{:S(2)}, u32[]{:S(2)}) collective-permute-start(f32[8,128]{1,0:T(8,128)S(1)} %bitcast.21), channel_id=1, source_target_pairs={{0,1},{1,2},{2,3},{3,4},{4,5},{5,6},{6,7},{7,8},{8,9},{9,10},{10,1... | collective-permute-start | bytes 12296 | tf_op jit(solution)/shard_map/ppermute | solution.py:177
  5.1 5.3 %collective-permute-start.1 = (f32[8,128]{1,0:T(8,128)S(1)}, f32[8,128]{1,0:T(8,128)S(1)}, u32[]{:S(2)}, u32[]{:S(2)}) collective-permute-start(f32[8,128]{1,0:T(8,128)S(1)} %bitcast.20), channel_id=1, source_target_pairs={{1,0},{2,1},{3,2},{4,3},{5,4},{6,5},{7,6},{8,7},{9,8},{10,9},{11,1... | collective-permute-start | bytes 12296 | tf_op jit(solution)/shard_map/ppermute | solution.py:178
  6.4 4.0 %collective-permute-start.2 = (f32[1,128,128]{2,1,0:T(8,128)}, f32[1,128,128]{2,1,0:T(8,128)S(1)}, u32[]{:S(2)}, u32[]{:S(2)}) collective-permute-start(f32[1,128,128]{2,1,0:T(8,128)} %area_ref.1), channel_id=1, source_target_pairs={{0,64},{64,0},{1,65},{65,1},{2,66},{66,2},{3,67},{67,3},{4,68},{68... | collective-permute-start | bytes 196616 | tf_op jit(solution)/shard_map/ppermute | solution.py:179
  8.2 1.0 %copy-start = (f32[1,8,128,128]{3,2,1,0:T(8,128)S(1)}, f32[1,8,128,128]{3,2,1,0:T(8,128)}, u32[]{:S(2)}) copy-start(f32[1,8,128,128]{3,2,1,0:T(8,128)} %surf_ref.1) | copy-start | bytes 1572868
  9.2 0.8 %copy-start.2 = (f32[1,128,128]{2,1,0:T(8,128)S(1)}, f32[1,128,128]{2,1,0:T(8,128)}, u32[]{:S(2)}) copy-start(f32[1,128,128]{2,1,0:T(8,128)} %area_ref.1) | copy-start | bytes 196612
  18.5 40.8 %copy-start.1 = (s32[128,128]{1,0:T(8,128)S(1)}, s32[128,128]{1,0:T(8,128)}, u32[]{:S(2)}) copy-start(s32[128,128]{1,0:T(8,128)} %sea_ref.3) | copy-start | bytes 196612
  60.5 18.9 %collective-permute-start.3 = (f32[8,128,128]{2,1,0:T(8,128)S(1)}, f32[8,128,128]{2,1,0:T(8,128)S(1)}, u32[]{:S(2)}, u32[]{:S(2)}) collective-permute-start(f32[8,128,128]{2,1,0:T(8,128)S(1)} %get-tuple-element.19), channel_id=1, source_target_pairs={{0,64},{64,0},{1,65},{65,1},{2,66},{66,2},{3,67},{67,3},{4,68},{68... | collective-permute-start | bytes 1572872 | tf_op jit(solution)/shard_map/ppermute | solution.py:234
  77.1 2.3 %collective-permute-start.4 = (f32[1,128]{1,0:T(1,128)S(1)}, f32[1,128]{1,0:T(1,128)S(1)}, u32[]{:S(2)}, u32[]{:S(2)}) collective-permute-start(f32[1,128]{1,0:T(1,128)S(1)} %bitcast.22), channel_id=1, source_target_pairs={{0,64},{64,0},{1,65},{65,1},{2,66},{66,2},{3,67},{67,3},{4,68},{68... | collective-permute-start | bytes 1544 | tf_op jit(solution)/shard_map/ppermute | solution.py:236

commit v4 on v3

--- a/solution.py
+++ b/solution.py
@@ -12,6 +12,7 @@
 SUB = 8
 CHUNKS = 8
 PIECES = 2
+EARLY = 4
 
 F32 = jnp.float32
 BF16 = jnp.bfloat16
@@ -33,13 +34,21 @@
 
 
 def prepare_kernel(
-    surf_ref, area_ref, smooth_ref, part_ref, rim_ref, *, fields, rows
+    code_ref, surf_ref, w_hbm,
+    smooth_ref, w_ref, spot_ref, targets_ref,
+    sems, *, blocks, fields, rows, slots, tiles,
 ):
+    size = w_ref.shape[0] // EARLY
+    copies = [
+        pltpu.make_async_copy(
+            w_hbm.at[0, pl.ds(p * size, size)], w_ref.at[pl.ds(p * size, size)], sems.at[p]
+        )
+        for p in range(EARLY)
+    ]
+    for copy in copies:
+        copy.start()
     r_iota = lax.broadcasted_iota(I32, (rows, LANES), 0)
     c_iota = lax.broadcasted_iota(I32, (rows, LANES), 1)
-    area = area_ref[0]
-    rim_ref[0:1, :] = area[0:1]
-    rim_ref[1:2, :] = area[rows - 1 : rows]
     for f in range(fields):
         s = surf_ref[0, f]
         n = jnp.where(r_iota > 0, pltpu.roll(s, 1, 0), 0.0)
@@ -47,54 +56,65 @@
         n += jnp.where(c_iota > 0, pltpu.roll(s, 1, 1), 0.0)
         n += jnp.where(c_iota < LANES - 1, pltpu.roll(s, LANES - 1, 1), 0.0)
         sm = s + RATE * (n - 4.0 * s)
-        part_ref[pl.ds(f, 1), :] = jnp.sum(area * sm, axis=0, keepdims=True)
         smooth_ref[pl.ds(f, rows, stride=fields), :] = sm
 
+    pitch = fields * slots + 1
+    code = code_ref[...]
+    tile = (code >> 14).astype(F32)
+    local = ((code >> 7) & (rows - 1)).astype(F32)
+
+    def column(v):
+        parts = [v[:, i : i + LANES] for i in range(0, blocks, LANES)]
+        return jnp.concatenate([jnp.broadcast_to(p, (LANES, LANES)).T for p in parts], axis=0)
+
+    def ones(mask):
+        return jnp.where(mask, 1.0, 0.0).astype(BF16)
+
+    def count(a, b):
+        return jnp.dot(a, b, preferred_element_type=F32)
+
+    down = lax.broadcasted_iota(I32, (blocks, blocks), 0)
+    right = lax.broadcasted_iota(I32, (blocks, blocks), 1)
+    same = jnp.concatenate([column(tile)] * (blocks // LANES), axis=1) == tile
+    rank = count(jnp.ones((SUB, blocks), BF16), ones(same & (down < right)))[0:1]
+    rank_down = count(ones(same & (right < down)), jnp.ones((blocks, LANES), BF16))
+    spot_ref[...] = ((code >> 14) * pitch + rank.astype(I32)) * rows + (code & (rows - 1))
+    tiles_down = lax.broadcasted_iota(I32, (tiles, blocks), 0).astype(F32)
+    lane = lax.broadcasted_iota(I32, (blocks, LANES), 1).astype(F32)
+    value = jnp.where(lane == rank_down, column(local) + 1.0, 0.0).astype(BF16)
+    targets_ref[...] = count(ones(tiles_down == tile), value) - 1.0
+
+    for copy in copies:
+        copy.wait()
+
 
 def products_kernel(
-    section_ref, code_ref, smooth_ref, part_ref, rim_ref, before_ref, after_ref, far_ref, w_hbm,
-    packed_ref, total_ref, area_ref,
-    spot_ref, count, index, wbuf, rows2, w_sems,
+    section_ref, spot_ref, targets_ref, smooth_ref, before_ref, after_ref, far_ref, early_ref,
+    w_hbm,
+    packed_ref, area_ref, rim_ref,
+    wbuf, rows2, w_sems,
     *, blocks, fields, rows, slots, tiles,
 ):
     per = blocks // CHUNKS
     pitch = fields * slots + 1
 
+    size = per // PIECES
+
     def fetch(p):
-        span = pl.ds(p * (per // PIECES), per // PIECES)
-        return pltpu.make_async_copy(w_hbm.at[0, span], wbuf.at[span], w_sems.at[p])
-
-    for p in range(CHUNKS * PIECES):
+        return pltpu.make_async_copy(
+            w_hbm.at[0, pl.ds(per + p * size, size)], wbuf.at[pl.ds(p * size, size)], w_sems.at[p]
+        )
+
+    for p in range((CHUNKS - 1) * PIECES):
         fetch(p).start()
 
     area_ref[...] = far_ref[...]
     before = RATE * before_ref[...]
     after = RATE * after_ref[...]
-    total_ref[...] = part_ref[...] + rim_ref[0:1] * before + rim_ref[1:2] * after
-
-    def clear(t, carry):
-        count[t] = 0
-        return carry
-
-    lax.fori_loop(0, tiles, clear, 0, unroll=8)
-    index[...] = jnp.full((tiles * slots, LANES), -1.0, F32)
-
-    def number(i, carry):
-        codes = [code_ref[0, i * SUB + j] for j in range(SUB)]
-        for j, code in enumerate(codes):
-            t = code >> 14
-            rank = count[t]
-            count[t] = rank + 1
-            spot_ref[i * SUB + j] = (t * pitch + rank) * rows + (code & (rows - 1))
-            local = jnp.full((1, LANES), (code >> 7) & (rows - 1), I32)
-            index[pl.ds(t * slots + rank, 1), :] = local.astype(F32)
-        return carry
-
-    lax.fori_loop(0, blocks // SUB, number, 0)
-    slot = lax.broadcasted_iota(I32, (tiles, slots, LANES), 1)
-    lane = lax.broadcasted_iota(I32, (tiles, slots, LANES), 2)
-    own = jnp.where(slot == lane, index[...].reshape(tiles, slots, LANES), 0.0)
-    packed_ref[pl.ds(fields * slots, tiles, stride=pitch), :] = jnp.sum(own, axis=1)
+    rim_ref[0] = before
+    rim_ref[1] = after
+
+    packed_ref[pl.ds(fields * slots, tiles, stride=pitch), :] = targets_ref[...]
 
     def halves(g, carry):
         rows2[g] = split_rows(smooth_ref[pl.ds(pl.multiple_of(g * SUB, SUB), SUB), :])
@@ -104,20 +124,24 @@
     rows2[0] = split_rows(smooth_ref[0:SUB, :] + before)
     rows2[rows - 1] = split_rows(smooth_ref[pl.ds((rows - 1) * SUB, SUB), :] + after)
 
-    def chunk(c, carry):
-        spots = [spot_ref[c * per + b] for b in range(per)]
+    def chunk(c, w_ref):
+        spots = [spot_ref[0, c * per + b] for b in range(per)]
+        for b, spot in enumerate(spots):
+            out = block_product(rows2[spot & (rows - 1)], w_ref[b])
+            packed_ref[pl.ds(spot >> 7, SUB, stride=slots), :] = out
+
+    def later(c, carry):
         for p in range(PIECES):
             fetch(c * PIECES + p).wait()
-        for b, spot in enumerate(spots):
-            out = block_product(rows2[spot & (rows - 1)], wbuf[c * per + b])
-            packed_ref[pl.ds(spot >> 7, SUB, stride=slots), :] = out
+        chunk(c + 1, wbuf.at[pl.ds(c * per, per)])
         return carry
 
-    lax.fori_loop(0, CHUNKS, chunk, 0)
+    chunk(0, early_ref)
+    lax.fori_loop(0, CHUNKS - 1, later, 0)
 
 
 def place_kernel(
-    section_ref, recv_ref, total_ref, area_ref, sea_ref, masked_ref, tail_ref,
+    section_ref, recv_ref, smooth_ref, rim_ref, own_ref, area_ref, sea_ref, masked_ref, tail_ref,
     *, fields, rows, slots, tiles,
 ):
     pitch = fields * slots + 1
@@ -130,6 +154,7 @@
     used = target >= 0.0
     mask = jnp.where(section_ref[0] == 1, 1.0, sea_ref[...].astype(F32))
     weight = area_ref[0] * mask
+    own = own_ref[0]
     lane1 = lax.broadcasted_iota(I32, (1, LANES), 1)
     tail = jnp.where(lane1 == fields, jnp.sum(weight), 0.0)
     for f in range(fields):
@@ -142,7 +167,9 @@
         got = jnp.dot(placing, lead, preferred_element_type=F32)
         got += jnp.dot(placing, rest, preferred_element_type=F32)
         masked_ref[f] = got * mask
-        gap = jnp.sum(total_ref[pl.ds(f, 1), :]) - jnp.sum(weight * got)
+        source = own * smooth_ref[pl.ds(f, rows, stride=fields), :]
+        edge = own[0:1] * rim_ref[0, f : f + 1] + own[rows - 1 : rows] * rim_ref[1, f : f + 1]
+        gap = jnp.sum(source - weight * got) + jnp.sum(edge)
         tail += jnp.where(lane1 == f, gap, 0.0)
     tail_ref[...] = jnp.broadcast_to(tail, (tiles, LANES))
 
@@ -180,41 +207,40 @@
     code = (dst_tile[:, :, 0] << 14) | (dst_local << 7) | src_row
 
     sizes = dict(blocks=blocks, fields=fields, rows=rows, slots=slots, tiles=tiles)
-    smooth, part, rim = pl.pallas_call(
-        functools.partial(prepare_kernel, fields=fields, rows=rows),
+    smooth, early, spot, targets = pl.pallas_call(
+        functools.partial(prepare_kernel, **sizes),
         out_shape=(
             jax.ShapeDtypeStruct((rows * fields, LANES), F32),
-            jax.ShapeDtypeStruct((fields, LANES), F32),
-            jax.ShapeDtypeStruct((SUB, LANES), F32),
+            jax.ShapeDtypeStruct((blocks // CHUNKS, cells, cells), F32),
+            jax.ShapeDtypeStruct((1, blocks), I32),
+            jax.ShapeDtypeStruct((tiles, LANES), F32),
         ),
-        in_specs=[VMEM, VMEM],
-        out_specs=(VMEM, VMEM, VMEM),
-        compiler_params=pltpu.CompilerParams(vmem_limit_bytes=8 << 20),
+        in_specs=[VMEM, VMEM, HBM],
+        out_specs=(VMEM,) * 4,
+        scratch_shapes=[pltpu.SemaphoreType.DMA((EARLY,))],
+        compiler_params=pltpu.CompilerParams(vmem_limit_bytes=46 << 20),
         cost_estimate=pl.CostEstimate(flops=10**7, bytes_accessed=8 << 20, transcendentals=0),
         name="prepare",
-    )(surface, area)
-
-    packed, total, area_far = pl.pallas_call(
+    )(code, surface, weights)
+
+    packed, area_far, rim = pl.pallas_call(
         functools.partial(products_kernel, **sizes),
         out_shape=(
             jax.ShapeDtypeStruct((tiles * pitch, LANES), F32),
-            jax.ShapeDtypeStruct((fields, LANES), F32),
             jax.ShapeDtypeStruct((1, rows, cells), F32),
+            jax.ShapeDtypeStruct((2, fields, LANES), F32),
         ),
         in_specs=[SMEM] * 2 + [VMEM] * 6 + [HBM],
         out_specs=(VMEM, VMEM, VMEM),
         scratch_shapes=[
-            pltpu.SMEM((blocks,), I32),
-            pltpu.SMEM((tiles,), I32),
-            pltpu.VMEM((tiles * slots, LANES), F32),
-            pltpu.VMEM((blocks, cells, cells), F32),
+            pltpu.VMEM((blocks - blocks // CHUNKS, cells, cells), F32),
             pltpu.VMEM((rows, 2 * SUB, cells), BF16),
-            pltpu.SemaphoreType.DMA((CHUNKS * PIECES,)),
+            pltpu.SemaphoreType.DMA(((CHUNKS - 1) * PIECES,)),
         ],
         compiler_params=pltpu.CompilerParams(vmem_limit_bytes=46 << 20),
         cost_estimate=pl.CostEstimate(flops=2 * 10**8, bytes_accessed=20 << 20, transcendentals=0),
         name="products",
-    )(section, code, smooth, part, rim, before, after, area_far, weights)
+    )(section, spot, targets, smooth, before, after, area_far, early, weights)
 
     flat = packed.reshape(tiles, 1, pitch * LANES)
     recv = lax.all_to_all(flat, "tile", 0, 0, tiled=True).reshape(tiles * pitch, LANES)
@@ -225,11 +251,11 @@
             jax.ShapeDtypeStruct((fields, rows, cells), F32),
             jax.ShapeDtypeStruct((tiles, LANES), F32),
         ),
-        in_specs=[SMEM, VMEM, VMEM, VMEM, VMEM],
+        in_specs=[SMEM] + [VMEM] * 6,
         out_specs=(VMEM, VMEM),
         compiler_params=pltpu.CompilerParams(vmem_limit_bytes=24 << 20),
         name="place",
-    )(section, recv, total, area_far, sea)
+    )(section, recv, smooth, rim, area, area_far, sea)
 
     masked = lax.ppermute(masked, "comp", swap)
     tail = lax.all_to_all(tail, "tile", 0, 0, tiled=True)

time: 80.9 us -> 79.9 us (0.988)
  local copies, waits for them, and re-layouts: 2.67 us -> 1.83 us
    pallas_call x1, Pallas kernels: 0.39 us -> 1.78 us  [shards(): pl.pallas_call(functools.partial(prepare_kernel, **sizes), out_shape=(jax...]
    pallas_call x1, Pallas kernels: 7.95 us -> 6.9 us  [shards(): pl.pallas_call(functools.partial(products_kernel, **sizes), out_shape=(ja...]
    unnamed x6, local copies, waits for them, and re-layouts: 1.89 us -> 1.05 us
  transfers between devices with their start and end apart: 5 -> 5, of which waited for: 1 -> 1; matrix products, arithmetic and copies ran while one was open for 1% -> 1% of each run, Pallas kernels for 0% -> 2%
where the time goes in v4:
time: 79.9 us; the launch traced here: 79.5 us
  blocking collectives  53.3 us (67%)
  starting transfers between devices  11.6 us (15%)
  Pallas kernels  11 us (14%)
  local copies, waits for them, and re-layouts  1.83 us (2%)
  waiting for transfers between devices  0.83 us (1%)
  other arithmetic  0.8 us (1%)
    all_to_all x1, blocking collectives, shards(): lax.all_to_all(flat, 'tile', 0, 0, tiled=True).reshape(tiles * pitch, LANES)  40.2 us
    all_to_all x1, blocking collectives, shards(): tail = lax.all_to_all(tail, 'tile', 0, 0, tiled=True)  13.1 us
    pallas_call x1, Pallas kernels, shards(): pl.pallas_call(functools.partial(products_kernel, **sizes), out_shape=(ja...  6.9 us
    ppermute x1, starting transfers between devices, shards(): before = lax.ppermute(surface[0, :, rows - 1], 'tile', up)  4.36 us
    ppermute x1, starting transfers between devices, shards(): masked = lax.ppermute(masked, 'comp', swap)  3.42 us
    pallas_call x1, Pallas kernels, shards(): pl.pallas_call(functools.partial(prepare_kernel, **sizes), out_shape=(jax...  1.78 us
  transfers between devices with their start and end apart: 5, of which 1 were waited for; matrix products, arithmetic and copies ran while one was open for 1% of the time, Pallas kernels for 2%

profile of v4, /device:TPU:1, one launch (start us, length us, event | category | flops | bytes accessed | tf_op | source)
XLA Modules:
  0.0 79.5 jit_solution(327142008746271687)
XLA Ops:
  0.0 0.8 fusion.1
  0.8 4.4 %collective-permute-start = (f32[8,128]{1,0:T(8,128)S(1)}, f32[8,128]{1,0:T(8,128)S(1)}, u32[]{:S(2)}, u32[]{:S(2)}) collective-permute-start(f32[8,128]{1,0:T(8,128)S(1)} %bitcast.21), channel_id=1, source_target_pairs={{0,1},{1,2},{2,3},{3,4},{4,5},{5,6},{6,7},{7,8},{8,9},{9,10},{10,1... | collective-permute-start | bytes 12296 | tf_op jit(solution)/shard_map/ppermute | solution.py:204
  5.1 1.3 %collective-permute-start.1 = (f32[8,128]{1,0:T(8,128)S(1)}, f32[8,128]{1,0:T(8,128)S(1)}, u32[]{:S(2)}, u32[]{:S(2)}) collective-permute-start(f32[8,128]{1,0:T(8,128)S(1)} %bitcast.20), channel_id=1, source_target_pairs={{1,0},{2,1},{3,2},{4,3},{5,4},{6,5},{7,6},{8,7},{9,8},{10,9},{11,1... | collective-permute-start | bytes 12296 | tf_op jit(solution)/shard_map/ppermute | solution.py:205
  6.4 1.0 %collective-permute-start.2 = (f32[1,128,128]{2,1,0:T(8,128)}, f32[1,128,128]{2,1,0:T(8,128)S(1)}, u32[]{:S(2)}, u32[]{:S(2)}) collective-permute-start(f32[1,128,128]{2,1,0:T(8,128)} %own_ref.1), channel_id=1, source_target_pairs={{0,64},{64,0},{1,65},{65,1},{2,66},{66,2},{3,67},{67,3},{4,68},{68... | collective-permute-start | bytes 196616 | tf_op jit(solution)/shard_map/ppermute | solution.py:206
  7.5 0.7 fusion.code_ref
  8.2 0.0 copy-start
  8.2 1.0 %copy-done = f32[1,8,128,128]{3,2,1,0:T(8,128)S(1)} copy-done((f32[1,8,128,128]{3,2,1,0:T(8,128)S(1)}, f32[1,8,128,128]{3,2,1,0:T(8,128)}, u32[]{:S(2)}) %copy-start) | copy-done | bytes 524312
  9.2 1.8 %prepare.1 = (f32[1024,128]{1,0:T(8,128)S(1)}, f32[32,128,128]{2,1,0:T(8,128)S(1)}, s32[1,256]{1,0:T(1,128)S(1)}, f32[64,128]{1,0:T(8,128)S(1)}) custom-call(s32[1,256]{1,0:T(1,128)S(1)} %fusion.code_ref, f32[1,8,128,128]{3,2,1,0:T(8,128)S(1)} %copy-done, f32[1,256,128,128]{3,2,1,0:T(8,128)} %w_hbm.3), custom_call_target="tpu_custom_call" | custom-call | flops 10000000 | bytes 8388608 | tf_op jit(solution)/shard_map/prepare/pallas_call | solution.py:210
  11.0 0.0 collective-permute-done.before_ref
  11.0 0.0 collective-permute-done.1.after_ref
  11.0 0.0 collective-permute-done.2.far_ref
  11.1 6.9 %products.1 = (f32[4160,128]{1,0:T(8,128)S(1)}, f32[1,128,128]{2,1,0:T(8,128)S(1)}, f32[2,8,128]{2,1,0:T(8,128)S(1)}) custom-call(s32[1]{0:T(128)} %bitcast.section_ref, s32[1,256]{1,0:T(1,128)S(1)} %get-tuple-element.14.spot_ref, f32[64,128]{1,0:T(8,128)S(1)} %get-tuple-element.15.targets_ref, f32[1024,128]{1,0:T(8,128)S(1)} %get-tuple-element.16.smooth_ref, ...), custom_call_target="tpu_custom_call" | custom-call | flops 200000000 | bytes 20971520 | tf_op jit(solution)/shard_map/products/pallas_call | solution.py:226
  18.0 0.0 copy-start.1
  18.0 0.0 copy-start.2
  18.0 40.2 %all_to_all.14 = f32[64,1,8320]{2,1,0:T(1,128)S(1)} all-to-all(f32[64,1,8320]{2,1,0:T(1,128)S(1)} %bitcast.18), channel_id=1, replica_groups=mesh['comp'=2,'tile'=64] {'tile'}, dimensions={0} | all-to-all | bytes 4259840 | tf_op jit(solution)/shard_map/all_to_all | solution.py:246
  58.2 0.0 copy-done.1
  58.2 0.0 copy-done.2
  58.2 1.3 %place.1 = (f32[8,128,128]{2,1,0:T(8,128)S(1)}, f32[64,128]{1,0:T(8,128)S(1)}) custom-call(s32[1]{0:T(128)} %bitcast.section_ref, f32[4160,128]{1,0:T(8,128)S(1)} %bitcast.17, f32[1024,128]{1,0:T(8,128)S(1)} %get-tuple-element.16.smooth_ref, f32[2,8,128]{2,1,0:T(8,128)S(1)} %get-tuple-element.19.rim_ref, f32[1,128,128]{2,1,0:T(8,128)S(1)} %copy-done.2, ...), custom_call_target="tpu_custom_call" | custom-call | tf_op jit(solution)/shard_map/place/pallas_call | solution.py:248
  59.6 3.4 %collective-permute-start.3 = (f32[8,128,128]{2,1,0:T(8,128)S(1)}, f32[8,128,128]{2,1,0:T(8,128)S(1)}, u32[]{:S(2)}, u32[]{:S(2)}) collective-permute-start(f32[8,128,128]{2,1,0:T(8,128)S(1)} %get-tuple-element.21), channel_id=1, source_target_pairs={{0,64},{64,0},{1,65},{65,1},{2,66},{66,2},{3,67},{67,3},{4,68},{68... | collective-permute-start | bytes 1572872 | tf_op jit(solution)/shard_map/ppermute | solution.py:260
  63.0 13.1 %all_to_all.15 = f32[64,1,128]{2,1,0:T(1,128)S(1)} all-to-all(f32[64,1,128]{2,1,0:T(1,128)S(1)} %bitcast.19), channel_id=1, replica_groups=mesh['comp'=2,'tile'=64] {'tile'}, dimensions={0} | all-to-all | bytes 65536 | tf_op jit(solution)/shard_map/all_to_all | solution.py:261
  76.0 0.1 reduce_sum.9
  76.1 1.5 %collective-permute-start.4 = (f32[1,128]{1,0:T(1,128)S(1)}, f32[1,128]{1,0:T(1,128)S(1)}, u32[]{:S(2)}, u32[]{:S(2)}) collective-permute-start(f32[1,128]{1,0:T(1,128)S(1)} %bitcast.22), channel_id=1, source_target_pairs={{0,64},{64,0},{1,65},{65,1},{2,66},{66,2},{3,67},{67,3},{4,68},{68... | collective-permute-start | bytes 1544 | tf_op jit(solution)/shard_map/ppermute | solution.py:262
  77.7 0.8 %collective-permute-done.4.sums_ref = f32[1,128]{1,0:T(1,128)S(1)} collective-permute-done((f32[1,128]{1,0:T(1,128)S(1)}, f32[1,128]{1,0:T(1,128)S(1)}, u32[]{:S(2)}, u32[]{:S(2)}) %collective-permute-start.4) | collective-permute-done | bytes 544 | tf_op jit(solution)/shard_map/ppermute | solution.py:262
  78.5 0.0 collective-permute-done.3.masked_ref
  78.5 1.0 %correct.1 = f32[1,8,128,128]{3,2,1,0:T(8,128)} custom-call(s32[1]{0:T(128)} %bitcast.section_ref, f32[8,128,128]{2,1,0:T(8,128)S(1)} %collective-permute-done.3.masked_ref, f32[1,128]{1,0:T(1,128)S(1)} %collective-permute-done.4.sums_ref, s32[128,128]{1,0:T(8,128)S(1)} %copy-done.1), custom_call_target="tpu_custom_call" | custom-call | tf_op jit(solution)/shard_map/correct/pallas_call | solution.py:264
Async XLA Ops:
  0.8 10.2 %collective-permute-start = (f32[8,128]{1,0:T(8,128)S(1)}, f32[8,128]{1,0:T(8,128)S(1)}, u32[]{:S(2)}, u32[]{:S(2)}) collective-permute-start(f32[8,128]{1,0:T(8,128)S(1)} %bitcast.21), channel_id=1, source_target_pairs={{0,1},{1,2},{2,3},{3,4},{4,5},{5,6},{6,7},{7,8},{8,9},{9,10},{10,1... | collective-permute-start | bytes 12296 | tf_op jit(solution)/shard_map/ppermute | solution.py:204
  5.1 5.9 %collective-permute-start.1 = (f32[8,128]{1,0:T(8,128)S(1)}, f32[8,128]{1,0:T(8,128)S(1)}, u32[]{:S(2)}, u32[]{:S(2)}) collective-permute-start(f32[8,128]{1,0:T(8,128)S(1)} %bitcast.20), channel_id=1, source_target_pairs={{1,0},{2,1},{3,2},{4,3},{5,4},{6,5},{7,6},{8,7},{9,8},{10,9},{11,1... | collective-permute-start | bytes 12296 | tf_op jit(solution)/shard_map/ppermute | solution.py:205
  6.4 4.6 %collective-permute-start.2 = (f32[1,128,128]{2,1,0:T(8,128)}, f32[1,128,128]{2,1,0:T(8,128)S(1)}, u32[]{:S(2)}, u32[]{:S(2)}) collective-permute-start(f32[1,128,128]{2,1,0:T(8,128)} %own_ref.1), channel_id=1, source_target_pairs={{0,64},{64,0},{1,65},{65,1},{2,66},{66,2},{3,67},{67,3},{4,68},{68... | collective-permute-start | bytes 196616 | tf_op jit(solution)/shard_map/ppermute | solution.py:206
  8.2 1.0 %copy-start = (f32[1,8,128,128]{3,2,1,0:T(8,128)S(1)}, f32[1,8,128,128]{3,2,1,0:T(8,128)}, u32[]{:S(2)}) copy-start(f32[1,8,128,128]{3,2,1,0:T(8,128)} %surf_ref.1) | copy-start | bytes 1572868
  18.0 40.2 %copy-start.1 = (s32[128,128]{1,0:T(8,128)S(1)}, s32[128,128]{1,0:T(8,128)}, u32[]{:S(2)}) copy-start(s32[128,128]{1,0:T(8,128)} %sea_ref.3) | copy-start | bytes 196612
  18.0 40.2 %copy-start.2 = (f32[1,128,128]{2,1,0:T(8,128)S(1)}, f32[1,128,128]{2,1,0:T(8,128)}, u32[]{:S(2)}) copy-start(f32[1,128,128]{2,1,0:T(8,128)} %own_ref.1) | copy-start | bytes 196612
  59.6 18.9 %collective-permute-start.3 = (f32[8,128,128]{2,1,0:T(8,128)S(1)}, f32[8,128,128]{2,1,0:T(8,128)S(1)}, u32[]{:S(2)}, u32[]{:S(2)}) collective-permute-start(f32[8,128,128]{2,1,0:T(8,128)S(1)} %get-tuple-element.21), channel_id=1, source_target_pairs={{0,64},{64,0},{1,65},{65,1},{2,66},{66,2},{3,67},{67,3},{4,68},{68... | collective-permute-start | bytes 1572872 | tf_op jit(solution)/shard_map/ppermute | solution.py:260
  76.1 2.3 %collective-permute-start.4 = (f32[1,128]{1,0:T(1,128)S(1)}, f32[1,128]{1,0:T(1,128)S(1)}, u32[]{:S(2)}, u32[]{:S(2)}) collective-permute-start(f32[1,128]{1,0:T(1,128)S(1)} %bitcast.22), channel_id=1, source_target_pairs={{0,64},{64,0},{1,65},{65,1},{2,66},{66,2},{3,67},{67,3},{4,68},{68... | collective-permute-start | bytes 1544 | tf_op jit(solution)/shard_map/ppermute | solution.py:262

commit v5 on v4

--- a/solution.py
+++ b/solution.py
@@ -171,11 +171,14 @@
         edge = own[0:1] * rim_ref[0, f : f + 1] + own[rows - 1 : rows] * rim_ref[1, f : f + 1]
         gap = jnp.sum(source - weight * got) + jnp.sum(edge)
         tail += jnp.where(lane1 == f, gap, 0.0)
-    tail_ref[...] = jnp.broadcast_to(tail, (tiles, LANES))
+    tail_ref[...] = jnp.broadcast_to(tail, (2 * tiles, LANES))
 
 
 def correct_kernel(section_ref, masked_ref, sums_ref, sea_ref, out_ref, *, fields):
-    sums = sums_ref[...]
+    half = sums_ref.shape[0] // 2
+    near = jnp.sum(sums_ref[0:half, :], axis=0, keepdims=True)
+    far = jnp.sum(sums_ref[half:, :], axis=0, keepdims=True)
+    sums = jnp.where(section_ref[0] == 0, far, near)
     lane1 = lax.broadcasted_iota(I32, (1, LANES), 1)
     whole = jnp.sum(jnp.where(lane1 == fields, sums, 0.0), axis=1, keepdims=True)
     deficit = sums / whole
@@ -249,7 +252,7 @@
         functools.partial(place_kernel, fields=fields, rows=rows, slots=slots, tiles=tiles),
         out_shape=(
             jax.ShapeDtypeStruct((fields, rows, cells), F32),
-            jax.ShapeDtypeStruct((tiles, LANES), F32),
+            jax.ShapeDtypeStruct((2 * tiles, LANES), F32),
         ),
         in_specs=[SMEM] + [VMEM] * 6,
         out_specs=(VMEM, VMEM),
@@ -258,8 +261,7 @@
     )(section, recv, smooth, rim, area, area_far, sea)
 
     masked = lax.ppermute(masked, "comp", swap)
-    tail = lax.all_to_all(tail, "tile", 0, 0, tiled=True)
-    sums = lax.ppermute(jnp.sum(tail, axis=0, keepdims=True), "comp", swap)
+    sums = lax.all_to_all(tail, ("comp", "tile"), 0, 0, tiled=True)
 
     return pl.pallas_call(
         functools.partial(correct_kernel, fields=fields),

time: 79.9 us -> 77.4 us (0.969)
  starting transfers between devices: 11.6 us -> 10.1 us
  waiting for transfers between devices: 0.83 us -> 0.01 us
    ppermute x1 -> x0, starting transfers between devices: 1.52 us -> none  [shards(): sums = lax.ppermute(jnp.sum(tail, axis=0, keepdims=True), 'comp', swap)]
    ppermute x1 -> x0, waiting for transfers between devices: 0.82 us -> none  [shards(): sums = lax.ppermute(jnp.sum(tail, axis=0, keepdims=True), 'comp', swap)]
  transfers between devices with their start and end apart: 5 -> 4, of which waited for: 1 -> 0; matrix products, arithmetic and copies ran while one was open for 1% -> 1% of each run, Pallas kernels for 2% -> 2%
where the time goes in v5:
time: 77.4 us; the launch traced here: 77 us
  blocking collectives  53.2 us (69%)
  Pallas kernels  11 us (14%)
  starting transfers between devices  10.1 us (13%)
  local copies, waits for them, and re-layouts  1.83 us (2%)
    all_to_all x1, blocking collectives, shards(): lax.all_to_all(flat, 'tile', 0, 0, tiled=True).reshape(tiles * pitch, LANES)  40.2 us
    all_to_all x1, blocking collectives, shards(): sums = lax.all_to_all(tail, ('comp', 'tile'), 0, 0, tiled=True)  13 us
    pallas_call x1, Pallas kernels, shards(): pl.pallas_call(functools.partial(products_kernel, **sizes), out_shape=(ja...  6.9 us
    ppermute x1, starting transfers between devices, shards(): before = lax.ppermute(surface[0, :, rows - 1], 'tile', up)  4.36 us
    ppermute x1, starting transfers between devices, shards(): masked = lax.ppermute(masked, 'comp', swap)  3.41 us
    pallas_call x1, Pallas kernels, shards(): pl.pallas_call(functools.partial(prepare_kernel, **sizes), out_shape=(jax...  1.78 us
  transfers between devices with their start and end apart: 4, of which 0 were waited for; matrix products, arithmetic and copies ran while one was open for 1% of the time, Pallas kernels for 2%

profile of v5, /device:TPU:1, one launch (start us, length us, event | category | flops | bytes accessed | tf_op | source)
XLA Modules:
  0.0 77.0 jit_solution(3222214851207308165)
XLA Ops:
  0.0 0.8 %fusion.1 = (f32[1,8,1,128]{3,2,1,0:T(1,128)S(1)}, f32[1,8,1,128]{3,2,1,0:T(1,128)S(1)}) fusion(f32[1,8,128,128]{3,2,1,0:T(8,128)} %surf_ref.1), kind=kLoop, calls=%fused_computation.2 | loop fusion | bytes 16384 | tf_op jit(solution)/shard_map/slice | solution.py:208
  0.8 4.4 %collective-permute-start = (f32[8,128]{1,0:T(8,128)S(1)}, f32[8,128]{1,0:T(8,128)S(1)}, u32[]{:S(2)}, u32[]{:S(2)}) collective-permute-start(f32[8,128]{1,0:T(8,128)S(1)} %bitcast.22), channel_id=1, source_target_pairs={{0,1},{1,2},{2,3},{3,4},{4,5},{5,6},{6,7},{7,8},{8,9},{9,10},{10,1... | collective-permute-start | bytes 12296 | tf_op jit(solution)/shard_map/ppermute | solution.py:207
  5.1 1.3 %collective-permute-start.1 = (f32[8,128]{1,0:T(8,128)S(1)}, f32[8,128]{1,0:T(8,128)S(1)}, u32[]{:S(2)}, u32[]{:S(2)}) collective-permute-start(f32[8,128]{1,0:T(8,128)S(1)} %bitcast.21), channel_id=1, source_target_pairs={{1,0},{2,1},{3,2},{4,3},{5,4},{6,5},{7,6},{8,7},{9,8},{10,9},{11,1... | collective-permute-start | bytes 12296 | tf_op jit(solution)/shard_map/ppermute | solution.py:208
  6.4 1.0 %collective-permute-start.2 = (f32[1,128,128]{2,1,0:T(8,128)}, f32[1,128,128]{2,1,0:T(8,128)S(1)}, u32[]{:S(2)}, u32[]{:S(2)}) collective-permute-start(f32[1,128,128]{2,1,0:T(8,128)} %own_ref.1), channel_id=1, source_target_pairs={{0,64},{64,0},{1,65},{65,1},{2,66},{66,2},{3,67},{67,3},{4,68},{68... | collective-permute-start | bytes 196616 | tf_op jit(solution)/shard_map/ppermute | solution.py:209
  7.5 0.7 fusion.code_ref
  8.2 0.0 copy-start
  8.2 1.0 %copy-done = f32[1,8,128,128]{3,2,1,0:T(8,128)S(1)} copy-done((f32[1,8,128,128]{3,2,1,0:T(8,128)S(1)}, f32[1,8,128,128]{3,2,1,0:T(8,128)}, u32[]{:S(2)}) %copy-start) | copy-done | bytes 524312
  9.2 1.8 %prepare.1 = (f32[1024,128]{1,0:T(8,128)S(1)}, f32[32,128,128]{2,1,0:T(8,128)S(1)}, s32[1,256]{1,0:T(1,128)S(1)}, f32[64,128]{1,0:T(8,128)S(1)}) custom-call(s32[1,256]{1,0:T(1,128)S(1)} %fusion.code_ref, f32[1,8,128,128]{3,2,1,0:T(8,128)S(1)} %copy-done, f32[1,256,128,128]{3,2,1,0:T(8,128)} %w_hbm.3), custom_call_target="tpu_custom_call" | custom-call | flops 10000000 | bytes 8388608 | tf_op jit(solution)/shard_map/prepare/pallas_call | solution.py:213
  11.0 0.0 collective-permute-done.before_ref
  11.0 0.0 collective-permute-done.1.after_ref
  11.0 0.0 collective-permute-done.2.far_ref
  11.1 6.9 %products.1 = (f32[4160,128]{1,0:T(8,128)S(1)}, f32[1,128,128]{2,1,0:T(8,128)S(1)}, f32[2,8,128]{2,1,0:T(8,128)S(1)}) custom-call(s32[1]{0:T(128)} %bitcast.section_ref, s32[1,256]{1,0:T(1,128)S(1)} %get-tuple-element.14.spot_ref, f32[64,128]{1,0:T(8,128)S(1)} %get-tuple-element.15.targets_ref, f32[1024,128]{1,0:T(8,128)S(1)} %get-tuple-element.16.smooth_ref, ...), custom_call_target="tpu_custom_call" | custom-call | flops 200000000 | bytes 20971520 | tf_op jit(solution)/shard_map/products/pallas_call | solution.py:229
  18.0 0.0 copy-start.1
  18.0 0.0 copy-start.2
  18.0 40.2 %all_to_all.16 = f32[64,1,8320]{2,1,0:T(1,128)S(1)} all-to-all(f32[64,1,8320]{2,1,0:T(1,128)S(1)} %bitcast.18), channel_id=1, replica_groups=mesh['comp'=2,'tile'=64] {'tile'}, dimensions={0} | all-to-all | bytes 4259840 | tf_op jit(solution)/shard_map/all_to_all | solution.py:249
  58.2 0.0 copy-done.1
  58.2 0.0 copy-done.2
  58.2 1.3 %place.1 = (f32[8,128,128]{2,1,0:T(8,128)S(1)}, f32[128,128]{1,0:T(8,128)S(1)}) custom-call(s32[1]{0:T(128)} %bitcast.section_ref, f32[4160,128]{1,0:T(8,128)S(1)} %bitcast.17, f32[1024,128]{1,0:T(8,128)S(1)} %get-tuple-element.16.smooth_ref, f32[2,8,128]{2,1,0:T(8,128)S(1)} %get-tuple-element.19.rim_ref, f32[1,128,128]{2,1,0:T(8,128)S(1)} %copy-done.2, ...), custom_call_target="tpu_custom_call" | custom-call | tf_op jit(solution)/shard_map/place/pallas_call | solution.py:251
  59.6 3.4 %collective-permute-start.3 = (f32[8,128,128]{2,1,0:T(8,128)S(1)}, f32[8,128,128]{2,1,0:T(8,128)S(1)}, u32[]{:S(2)}, u32[]{:S(2)}) collective-permute-start(f32[8,128,128]{2,1,0:T(8,128)S(1)} %get-tuple-element.21), channel_id=1, source_target_pairs={{0,64},{64,0},{1,65},{65,1},{2,66},{66,2},{3,67},{67,3},{4,68},{68... | collective-permute-start | bytes 1572872 | tf_op jit(solution)/shard_map/ppermute | solution.py:263
  63.0 13.0 %all_to_all.17 = f32[128,1,128]{2,1,0:T(1,128)S(1)} all-to-all(f32[128,1,128]{2,1,0:T(1,128)S(1)} %bitcast.20), channel_id=1, replica_groups=mesh['comp'=2,'tile'=64] {'comp','tile'}, dimensions={0} | all-to-all | bytes 131072 | tf_op jit(solution)/shard_map/all_to_all | solution.py:264
  76.0 0.0 collective-permute-done.3.masked_ref
  76.0 1.0 %correct.1 = f32[1,8,128,128]{3,2,1,0:T(8,128)} custom-call(s32[1]{0:T(128)} %bitcast.section_ref, f32[8,128,128]{2,1,0:T(8,128)S(1)} %collective-permute-done.3.masked_ref, f32[128,128]{1,0:T(8,128)S(1)} %bitcast.19, s32[128,128]{1,0:T(8,128)S(1)} %copy-done.1), custom_call_target="tpu_custom_call" | custom-call | tf_op jit(solution)/shard_map/correct/pallas_call | solution.py:266
Async XLA Ops:
  0.8 10.2 %collective-permute-start = (f32[8,128]{1,0:T(8,128)S(1)}, f32[8,128]{1,0:T(8,128)S(1)}, u32[]{:S(2)}, u32[]{:S(2)}) collective-permute-start(f32[8,128]{1,0:T(8,128)S(1)} %bitcast.22), channel_id=1, source_target_pairs={{0,1},{1,2},{2,3},{3,4},{4,5},{5,6},{6,7},{7,8},{8,9},{9,10},{10,1... | collective-permute-start | bytes 12296 | tf_op jit(solution)/shard_map/ppermute | solution.py:207
  5.1 5.9 %collective-permute-start.1 = (f32[8,128]{1,0:T(8,128)S(1)}, f32[8,128]{1,0:T(8,128)S(1)}, u32[]{:S(2)}, u32[]{:S(2)}) collective-permute-start(f32[8,128]{1,0:T(8,128)S(1)} %bitcast.21), channel_id=1, source_target_pairs={{1,0},{2,1},{3,2},{4,3},{5,4},{6,5},{7,6},{8,7},{9,8},{10,9},{11,1... | collective-permute-start | bytes 12296 | tf_op jit(solution)/shard_map/ppermute | solution.py:208
  6.4 4.6 %collective-permute-start.2 = (f32[1,128,128]{2,1,0:T(8,128)}, f32[1,128,128]{2,1,0:T(8,128)S(1)}, u32[]{:S(2)}, u32[]{:S(2)}) collective-permute-start(f32[1,128,128]{2,1,0:T(8,128)} %own_ref.1), channel_id=1, source_target_pairs={{0,64},{64,0},{1,65},{65,1},{2,66},{66,2},{3,67},{67,3},{4,68},{68... | collective-permute-start | bytes 196616 | tf_op jit(solution)/shard_map/ppermute | solution.py:209
  8.2 1.0 %copy-start = (f32[1,8,128,128]{3,2,1,0:T(8,128)S(1)}, f32[1,8,128,128]{3,2,1,0:T(8,128)}, u32[]{:S(2)}) copy-start(f32[1,8,128,128]{3,2,1,0:T(8,128)} %surf_ref.1) | copy-start | bytes 1572868
  18.0 40.2 %copy-start.1 = (s32[128,128]{1,0:T(8,128)S(1)}, s32[128,128]{1,0:T(8,128)}, u32[]{:S(2)}) copy-start(s32[128,128]{1,0:T(8,128)} %sea_ref.3) | copy-start | bytes 196612
  18.0 40.2 %copy-start.2 = (f32[1,128,128]{2,1,0:T(8,128)S(1)}, f32[1,128,128]{2,1,0:T(8,128)}, u32[]{:S(2)}) copy-start(f32[1,128,128]{2,1,0:T(8,128)} %own_ref.1) | copy-start | bytes 196612
  59.6 16.4 %collective-permute-start.3 = (f32[8,128,128]{2,1,0:T(8,128)S(1)}, f32[8,128,128]{2,1,0:T(8,128)S(1)}, u32[]{:S(2)}, u32[]{:S(2)}) collective-permute-start(f32[8,128,128]{2,1,0:T(8,128)S(1)} %get-tuple-element.21), channel_id=1, source_target_pairs={{0,64},{64,0},{1,65},{65,1},{2,66},{66,2},{3,67},{67,3},{4,68},{68... | collective-permute-start | bytes 1572872 | tf_op jit(solution)/shard_map/ppermute | solution.py:263

commit v6 on v5

--- a/solution.py
+++ b/solution.py
@@ -155,8 +155,7 @@
     mask = jnp.where(section_ref[0] == 1, 1.0, sea_ref[...].astype(F32))
     weight = area_ref[0] * mask
     own = own_ref[0]
-    lane1 = lax.broadcasted_iota(I32, (1, LANES), 1)
-    tail = jnp.where(lane1 == fields, jnp.sum(weight), 0.0)
+    gaps = []
     for f in range(fields):
         x = jnp.concatenate(
             [recv_ref[pl.ds(f * slots + j, tiles, stride=pitch), :] for j in range(slots)], axis=0
@@ -169,8 +168,13 @@
         masked_ref[f] = got * mask
         source = own * smooth_ref[pl.ds(f, rows, stride=fields), :]
         edge = own[0:1] * rim_ref[0, f : f + 1] + own[rows - 1 : rows] * rim_ref[1, f : f + 1]
-        gap = jnp.sum(source - weight * got) + jnp.sum(edge)
-        tail += jnp.where(lane1 == f, gap, 0.0)
+        gaps.append(jnp.sum(source - weight * got, axis=0, keepdims=True) + edge)
+    gaps.append(jnp.sum(weight, axis=0, keepdims=True))
+    gaps.append(jnp.zeros((2 * SUB - len(gaps), LANES), F32))
+    sums = jnp.sum(jnp.concatenate(gaps, axis=0), axis=1, keepdims=True)
+    down = lax.broadcasted_iota(I32, (2 * SUB, LANES), 0)
+    right = lax.broadcasted_iota(I32, (2 * SUB, LANES), 1)
+    tail = jnp.sum(jnp.where(down == right, sums, 0.0), axis=0, keepdims=True)
     tail_ref[...] = jnp.broadcast_to(tail, (2 * tiles, LANES))
 
 

time: 77.4 us -> 77.3 us (level)
  no operation moved by 1% of the time
where the time goes in v6:
time: 77.3 us; the launch traced here: 76.9 us
  blocking collectives  53.2 us (69%)
  Pallas kernels  11 us (14%)
  starting transfers between devices  10.1 us (13%)
  local copies, waits for them, and re-layouts  1.83 us (2%)
    all_to_all x1, blocking collectives, shards(): lax.all_to_all(flat, 'tile', 0, 0, tiled=True).reshape(tiles * pitch, LANES)  40.2 us
    all_to_all x1, blocking collectives, shards(): sums = lax.all_to_all(tail, ('comp', 'tile'), 0, 0, tiled=True)  13 us
    pallas_call x1, Pallas kernels, shards(): pl.pallas_call(functools.partial(products_kernel, **sizes), out_shape=(ja...  6.9 us
    ppermute x1, starting transfers between devices, shards(): before = lax.ppermute(surface[0, :, rows - 1], 'tile', up)  4.36 us
    ppermute x1, starting transfers between devices, shards(): masked = lax.ppermute(masked, 'comp', swap)  3.4 us
    pallas_call x1, Pallas kernels, shards(): pl.pallas_call(functools.partial(prepare_kernel, **sizes), out_shape=(jax...  1.78 us
  transfers between devices with their start and end apart: 4, of which 0 were waited for; matrix products, arithmetic and copies ran while one was open for 1% of the time, Pallas kernels for 2%

profile of v6, /device:TPU:1, one launch (start us, length us, event | category | flops | bytes accessed | tf_op | source)
XLA Modules:
  0.0 76.9 jit_solution(6944166654717167015)
XLA Ops:
  0.0 0.8 %fusion.1 = (f32[1,8,1,128]{3,2,1,0:T(1,128)S(1)}, f32[1,8,1,128]{3,2,1,0:T(1,128)S(1)}) fusion(f32[1,8,128,128]{3,2,1,0:T(8,128)} %surf_ref.1), kind=kLoop, calls=%fused_computation.2 | loop fusion | bytes 16384 | tf_op jit(solution)/shard_map/slice | solution.py:212
  0.8 4.4 %collective-permute-start = (f32[8,128]{1,0:T(8,128)S(1)}, f32[8,128]{1,0:T(8,128)S(1)}, u32[]{:S(2)}, u32[]{:S(2)}) collective-permute-start(f32[8,128]{1,0:T(8,128)S(1)} %bitcast.22), channel_id=1, source_target_pairs={{0,1},{1,2},{2,3},{3,4},{4,5},{5,6},{6,7},{7,8},{8,9},{9,10},{10,1... | collective-permute-start | bytes 12296 | tf_op jit(solution)/shard_map/ppermute | solution.py:211
  5.1 1.3 %collective-permute-start.1 = (f32[8,128]{1,0:T(8,128)S(1)}, f32[8,128]{1,0:T(8,128)S(1)}, u32[]{:S(2)}, u32[]{:S(2)}) collective-permute-start(f32[8,128]{1,0:T(8,128)S(1)} %bitcast.21), channel_id=1, source_target_pairs={{1,0},{2,1},{3,2},{4,3},{5,4},{6,5},{7,6},{8,7},{9,8},{10,9},{11,1... | collective-permute-start | bytes 12296 | tf_op jit(solution)/shard_map/ppermute | solution.py:212
  6.4 1.0 %collective-permute-start.2 = (f32[1,128,128]{2,1,0:T(8,128)}, f32[1,128,128]{2,1,0:T(8,128)S(1)}, u32[]{:S(2)}, u32[]{:S(2)}) collective-permute-start(f32[1,128,128]{2,1,0:T(8,128)} %own_ref.1), channel_id=1, source_target_pairs={{0,64},{64,0},{1,65},{65,1},{2,66},{66,2},{3,67},{67,3},{4,68},{68... | collective-permute-start | bytes 196616 | tf_op jit(solution)/shard_map/ppermute | solution.py:213
  7.5 0.7 fusion.code_ref
  8.2 0.0 copy-start
  8.2 1.0 %copy-done = f32[1,8,128,128]{3,2,1,0:T(8,128)S(1)} copy-done((f32[1,8,128,128]{3,2,1,0:T(8,128)S(1)}, f32[1,8,128,128]{3,2,1,0:T(8,128)}, u32[]{:S(2)}) %copy-start) | copy-done | bytes 524312
  9.2 1.8 %prepare.1 = (f32[1024,128]{1,0:T(8,128)S(1)}, f32[32,128,128]{2,1,0:T(8,128)S(1)}, s32[1,256]{1,0:T(1,128)S(1)}, f32[64,128]{1,0:T(8,128)S(1)}) custom-call(s32[1,256]{1,0:T(1,128)S(1)} %fusion.code_ref, f32[1,8,128,128]{3,2,1,0:T(8,128)S(1)} %copy-done, f32[1,256,128,128]{3,2,1,0:T(8,128)} %w_hbm.3), custom_call_target="tpu_custom_call" | custom-call | flops 10000000 | bytes 8388608 | tf_op jit(solution)/shard_map/prepare/pallas_call | solution.py:217
  11.0 0.0 collective-permute-done.before_ref
  11.0 0.0 collective-permute-done.1.after_ref
  11.0 0.0 collective-permute-done.2.far_ref
  11.1 6.9 %products.1 = (f32[4160,128]{1,0:T(8,128)S(1)}, f32[1,128,128]{2,1,0:T(8,128)S(1)}, f32[2,8,128]{2,1,0:T(8,128)S(1)}) custom-call(s32[1]{0:T(128)} %bitcast.section_ref, s32[1,256]{1,0:T(1,128)S(1)} %get-tuple-element.14.spot_ref, f32[64,128]{1,0:T(8,128)S(1)} %get-tuple-element.15.targets_ref, f32[1024,128]{1,0:T(8,128)S(1)} %get-tuple-element.16.smooth_ref, ...), custom_call_target="tpu_custom_call" | custom-call | flops 200000000 | bytes 20971520 | tf_op jit(solution)/shard_map/products/pallas_call | solution.py:233
  18.0 0.0 copy-start.1
  18.0 0.0 copy-start.2
  18.0 40.2 %all_to_all.16 = f32[64,1,8320]{2,1,0:T(1,128)S(1)} all-to-all(f32[64,1,8320]{2,1,0:T(1,128)S(1)} %bitcast.18), channel_id=1, replica_groups=mesh['comp'=2,'tile'=64] {'tile'}, dimensions={0} | all-to-all | bytes 4259840 | tf_op jit(solution)/shard_map/all_to_all | solution.py:253
  58.2 0.0 copy-done.1
  58.2 0.0 copy-done.2
  58.2 1.3 %place.1 = (f32[8,128,128]{2,1,0:T(8,128)S(1)}, f32[128,128]{1,0:T(8,128)S(1)}) custom-call(s32[1]{0:T(128)} %bitcast.section_ref, f32[4160,128]{1,0:T(8,128)S(1)} %bitcast.17, f32[1024,128]{1,0:T(8,128)S(1)} %get-tuple-element.16.smooth_ref, f32[2,8,128]{2,1,0:T(8,128)S(1)} %get-tuple-element.19.rim_ref, f32[1,128,128]{2,1,0:T(8,128)S(1)} %copy-done.2, ...), custom_call_target="tpu_custom_call" | custom-call | tf_op jit(solution)/shard_map/place/pallas_call | solution.py:255
  59.5 3.4 %collective-permute-start.3 = (f32[8,128,128]{2,1,0:T(8,128)S(1)}, f32[8,128,128]{2,1,0:T(8,128)S(1)}, u32[]{:S(2)}, u32[]{:S(2)}) collective-permute-start(f32[8,128,128]{2,1,0:T(8,128)S(1)} %get-tuple-element.21), channel_id=1, source_target_pairs={{0,64},{64,0},{1,65},{65,1},{2,66},{66,2},{3,67},{67,3},{4,68},{68... | collective-permute-start | bytes 1572872 | tf_op jit(solution)/shard_map/ppermute | solution.py:267
  62.9 13.0 %all_to_all.17 = f32[128,1,128]{2,1,0:T(1,128)S(1)} all-to-all(f32[128,1,128]{2,1,0:T(1,128)S(1)} %bitcast.20), channel_id=1, replica_groups=mesh['comp'=2,'tile'=64] {'comp','tile'}, dimensions={0} | all-to-all | bytes 131072 | tf_op jit(solution)/shard_map/all_to_all | solution.py:268
  75.9 0.0 collective-permute-done.3.masked_ref
  75.9 1.0 %correct.1 = f32[1,8,128,128]{3,2,1,0:T(8,128)} custom-call(s32[1]{0:T(128)} %bitcast.section_ref, f32[8,128,128]{2,1,0:T(8,128)S(1)} %collective-permute-done.3.masked_ref, f32[128,128]{1,0:T(8,128)S(1)} %bitcast.19, s32[128,128]{1,0:T(8,128)S(1)} %copy-done.1), custom_call_target="tpu_custom_call" | custom-call | tf_op jit(solution)/shard_map/correct/pallas_call | solution.py:270
Async XLA Ops:
  0.8 10.2 %collective-permute-start = (f32[8,128]{1,0:T(8,128)S(1)}, f32[8,128]{1,0:T(8,128)S(1)}, u32[]{:S(2)}, u32[]{:S(2)}) collective-permute-start(f32[8,128]{1,0:T(8,128)S(1)} %bitcast.22), channel_id=1, source_target_pairs={{0,1},{1,2},{2,3},{3,4},{4,5},{5,6},{6,7},{7,8},{8,9},{9,10},{10,1... | collective-permute-start | bytes 12296 | tf_op jit(solution)/shard_map/ppermute | solution.py:211
  5.1 5.9 %collective-permute-start.1 = (f32[8,128]{1,0:T(8,128)S(1)}, f32[8,128]{1,0:T(8,128)S(1)}, u32[]{:S(2)}, u32[]{:S(2)}) collective-permute-start(f32[8,128]{1,0:T(8,128)S(1)} %bitcast.21), channel_id=1, source_target_pairs={{1,0},{2,1},{3,2},{4,3},{5,4},{6,5},{7,6},{8,7},{9,8},{10,9},{11,1... | collective-permute-start | bytes 12296 | tf_op jit(solution)/shard_map/ppermute | solution.py:212
  6.4 4.6 %collective-permute-start.2 = (f32[1,128,128]{2,1,0:T(8,128)}, f32[1,128,128]{2,1,0:T(8,128)S(1)}, u32[]{:S(2)}, u32[]{:S(2)}) collective-permute-start(f32[1,128,128]{2,1,0:T(8,128)} %own_ref.1), channel_id=1, source_target_pairs={{0,64},{64,0},{1,65},{65,1},{2,66},{66,2},{3,67},{67,3},{4,68},{68... | collective-permute-start | bytes 196616 | tf_op jit(solution)/shard_map/ppermute | solution.py:213
  8.2 1.0 %copy-start = (f32[1,8,128,128]{3,2,1,0:T(8,128)S(1)}, f32[1,8,128,128]{3,2,1,0:T(8,128)}, u32[]{:S(2)}) copy-start(f32[1,8,128,128]{3,2,1,0:T(8,128)} %surf_ref.1) | copy-start | bytes 1572868
  18.0 40.2 %copy-start.1 = (s32[128,128]{1,0:T(8,128)S(1)}, s32[128,128]{1,0:T(8,128)}, u32[]{:S(2)}) copy-start(s32[128,128]{1,0:T(8,128)} %sea_ref.3) | copy-start | bytes 196612
  18.0 40.2 %copy-start.2 = (f32[1,128,128]{2,1,0:T(8,128)S(1)}, f32[1,128,128]{2,1,0:T(8,128)}, u32[]{:S(2)}) copy-start(f32[1,128,128]{2,1,0:T(8,128)} %own_ref.1) | copy-start | bytes 196612
  59.5 16.4 %collective-permute-start.3 = (f32[8,128,128]{2,1,0:T(8,128)S(1)}, f32[8,128,128]{2,1,0:T(8,128)S(1)}, u32[]{:S(2)}, u32[]{:S(2)}) collective-permute-start(f32[8,128,128]{2,1,0:T(8,128)S(1)} %get-tuple-element.21), channel_id=1, source_target_pairs={{0,64},{64,0},{1,65},{65,1},{2,66},{66,2},{3,67},{67,3},{4,68},{68... | collective-permute-start | bytes 1572872 | tf_op jit(solution)/shard_map/ppermute | solution.py:267
